TPU v7x, 128 devices: a whole 4x4x4 slice. The times are simulated.
128 devices in a mesh: grp: 4 (over x), dev: 32 (over z, y, core).
Axes of the slice: x: 4, y: 4, z: 4, core: 2. Of those that a mesh axis runs over, the one named last changes fastest.
Arguments:
- populations: float32 [512, 19, 4096], P(('grp', 'dev')), may hold values from 0.02 to 2.1
- solidity: float32 [512, 4096], P(('grp', 'dev')), may hold values from 0 to 1
- home_count: int32 [4, 8, 4], P('grp'), may hold values from 1 to 4, 8 in all within a row
Outputs:
- evolved: float32 [256, 19, 4096], P(('grp', 'dev'))
Inputs may be any that keep to these rules, and one draw needn't show every extreme that they name: `home_count`: each row of 4 counts sums to 8.
All inputs are finite; a program needn't handle non-finite values.
Results may differ from a plain program's by a relative error of at most 0.0001.
Values sent between devices are 32-bit elements; how exact they have to be, the bound alone decides.
A program may use at most 64 MiB of HBM per device.

v0:
```python
import jax
import jax.numpy as jnp
import numpy as np
from jax import lax
from jax.sharding import PartitionSpec as P

B = 16
AVG = 2
HS = 4
TEAM = 4
Q = 19
STEPS = 2


speeds = np.array(
    [
        [0, 0, 0],
        [1, 0, 0],
        [-1, 0, 0],
        [0, 1, 0],
        [0, -1, 0],
        [0, 0, 1],
        [0, 0, -1],
        [1, 1, 0],
        [-1, -1, 0],
        [1, -1, 0],
        [-1, 1, 0],
        [1, 0, 1],
        [-1, 0, -1],
        [1, 0, -1],
        [-1, 0, 1],
        [0, 1, 1],
        [0, -1, -1],
        [0, 1, -1],
        [0, -1, 1],
    ]
)
mirror = [0, 2, 1, 4, 3, 6, 5, 8, 7, 10, 9, 12, 11, 14, 13, 16, 15, 18, 17]
relax_rates = [
    0.0,
    1.19,
    1.4,
    0.0,
    1.2,
    0.0,
    1.2,
    0.0,
    1.2,
    1.25,
    1.4,
    1.25,
    1.4,
    1.25,
    1.25,
    1.25,
    1.98,
    1.98,
    1.98,
]
rest_density = 3.0
crossing = [1, 2, 7, 8, 9, 10, 11, 12, 13, 14]
rising_z = [5, 11, 14, 15, 18]
falling_z = [6, 12, 13, 16, 17]


def shifted_2(value, axis, steps):
    count = lax.axis_size(axis)
    pairs = [(source, (source + steps) % count) for source in range(count)]
    return lax.ppermute(value, axis, pairs)


def extended(cells, sides, width):
    for axis, dim in sides:
        count = lax.axis_size(axis)
        head = lax.slice_in_dim(cells, 0, width, axis=dim)
        tail = lax.slice_in_dim(cells, cells.shape[dim] - width, cells.shape[dim], axis=dim)
        cells = jnp.concatenate(
            [
                lax.ppermute(tail, axis, [(i, (i + 1) % count) for i in range(count)]),
                cells,
                lax.ppermute(head, axis, [((i + 1) % count, i) for i in range(count)]),
            ],
            axis=dim,
        )
    return cells


def moment_table():
    along_x = speeds[:, 0] * 1.0
    along_y = speeds[:, 1] * 1.0
    along_z = speeds[:, 2] * 1.0
    squared = along_x * along_x + along_y * along_y + along_z * along_z
    moment_rows = [
        np.ones(19),
        19 * squared - 30,
        (21 * squared * squared - 53 * squared + 24) / 2,
        along_x,
        (5 * squared - 9) * along_x,
        along_y,
        (5 * squared - 9) * along_y,
        along_z,
        (5 * squared - 9) * along_z,
        3 * along_x * along_x - squared,
        (3 * squared - 5) * (3 * along_x * along_x - squared),
        along_y * along_y - along_z * along_z,
        (3 * squared - 5) * (along_y * along_y - along_z * along_z),
        along_x * along_y,
        along_y * along_z,
        along_x * along_z,
        (along_y * along_y - along_z * along_z) * along_x,
        (along_z * along_z - along_x * along_x) * along_y,
        (along_x * along_x - along_y * along_y) * along_z,
    ]
    forward = np.stack(moment_rows)
    inverse = forward.T / np.sum(forward * forward, axis=1)[None, :]
    return (jnp.asarray(forward, jnp.float32), jnp.asarray(inverse, jnp.float32))


def collide(flat_cells, solid_flat):
    forward, inverse = moment_table()
    moments = jnp.dot(
        forward, flat_cells, precision=lax.Precision.HIGHEST, preferred_element_type=jnp.float32
    )
    density = moments[0]
    flux_x = moments[3]
    flux_y = moments[5]
    flux_z = moments[7]
    square = flux_x * flux_x + flux_y * flux_y + flux_z * flux_z
    stress_xx = (3.0 * flux_x * flux_x - square) / rest_density
    stress_ww = (flux_y * flux_y - flux_z * flux_z) / rest_density
    nothing = jnp.zeros_like(density)
    balance = jnp.stack(
        [
            density,
            -11.0 * density + 19.0 * square / rest_density,
            3.0 * density - 5.5 * square / rest_density,
            flux_x,
            -2.0 / 3.0 * flux_x,
            flux_y,
            -2.0 / 3.0 * flux_y,
            flux_z,
            -2.0 / 3.0 * flux_z,
            stress_xx,
            -0.5 * stress_xx,
            stress_ww,
            -0.5 * stress_ww,
            flux_x * flux_y / rest_density,
            flux_y * flux_z / rest_density,
            flux_x * flux_z / rest_density,
            nothing,
            nothing,
            nothing,
        ]
    )
    relax_table = jnp.asarray(np.array(relax_rates), jnp.float32)[:, None]
    relaxed = moments - relax_table * (moments - balance)
    collided = jnp.dot(
        inverse, relaxed, precision=lax.Precision.HIGHEST, preferred_element_type=jnp.float32
    )
    reflected = jnp.stack([flat_cells[index] for index in mirror])
    solid_share = solid_flat[None]
    return (1.0 - solid_share) * collided + solid_share * reflected


def ordered(selected, length):
    candidates = jnp.arange(selected.shape[0], dtype=jnp.int32)
    sort_keys = jnp.where(selected, candidates, candidates + selected.shape[0])
    picked = jnp.sort(sort_keys)[:length]
    return jnp.where(picked < selected.shape[0], picked, -1).astype(jnp.int32)


def find_places(pool_ids, wanted):
    matches = (pool_ids[None, :] == wanted[:, None]) & (wanted[:, None] >= 0)
    return jnp.argmax(matches, axis=1).astype(jnp.int32)


def on_device(populations, solidity, home_count):
    device = lax.axis_index("dev")
    member = device % TEAM
    team_index = device // TEAM
    counts_row = lax.dynamic_index_in_dim(home_count[0], team_index, 0, keepdims=False)
    inclusive = jnp.cumsum(counts_row).astype(jnp.int32)
    everyone = jnp.arange(TEAM * AVG, dtype=jnp.int32)
    holder = jnp.sum((inclusive[None, :] <= everyone[:, None]).astype(jnp.int32), axis=1)
    target = everyone // AVG
    home_ids = ordered(holder == member, HS)
    final_ids = member * AVG + jnp.arange(AVG, dtype=jnp.int32)
    pool_ids = [home_ids]
    pool_cells = [populations]
    pool_solid = [solidity]
    for offset in range(1 - TEAM, TEAM):
        if offset != 0:
            outgoing = ordered((holder == member) & (target == member + offset), AVG)
            places = find_places(home_ids, outgoing)
            outbound = (jnp.take(populations, places, axis=0), jnp.take(solidity, places, axis=0))
            came_cells, came_solid = shifted_2((outbound[0], outbound[1]), "dev", offset)
            source = member - offset
            pool_ids.append(ordered((holder == source) & (target == member), AVG))
            pool_cells.append(came_cells)
            pool_solid.append(came_solid)
    places = find_places(jnp.concatenate(pool_ids), final_ids)
    kept_cells = jnp.take(jnp.concatenate(pool_cells, axis=0), places, axis=0)
    kept_solid = jnp.take(jnp.concatenate(pool_solid, axis=0), places, axis=0)
    depth_z = AVG * B
    plane = B * depth_z
    lattice = kept_cells.reshape(AVG, Q, B, B, B).transpose(1, 2, 3, 0, 4).reshape(Q, B, plane)
    solid_part = kept_solid.reshape(AVG, B, B, B).transpose(1, 2, 0, 3).reshape(B * plane)
    z_position = jnp.arange(plane, dtype=jnp.int32) % depth_z
    at_bottom = (z_position == 0)[None, :]
    at_top = (z_position == depth_z - 1)[None, :]
    for repeat in range(STEPS):
        collided = collide(lattice.reshape(Q, B * plane), solid_part).reshape(Q, B, plane)
        moved_x = {}
        moving = collided[np.array(crossing)]
        widened = extended(moving, (("grp", 1),), 1)
        for place, direction in enumerate(crossing):
            step_x = int(speeds[direction, 0])
            moved_x[direction] = widened[place, 1 - step_x : 1 - step_x + B]
        for direction in range(19):
            if int(speeds[direction, 0]) == 0:
                moved_x[direction] = collided[direction]
        top_faces = jnp.stack(
            [moved_x[d].reshape(B, B, depth_z)[:, :, depth_z - 1] for d in rising_z]
        )
        bottom_faces = jnp.stack([moved_x[d].reshape(B, B, depth_z)[:, :, 0] for d in falling_z])
        below_z = shifted_2(top_faces, "dev", 1)
        above_z = shifted_2(bottom_faces, "dev", -1)
        shifted = []
        for direction in range(19):
            step_y = int(speeds[direction, 1])
            step_z = int(speeds[direction, 2])
            placed = moved_x[direction]
            if step_z == 1:
                rim = jnp.repeat(below_z[rising_z.index(direction)], depth_z, axis=1)
                placed = jnp.where(at_bottom, rim, jnp.roll(placed, 1, axis=1))
            elif step_z == -1:
                rim = jnp.repeat(above_z[falling_z.index(direction)], depth_z, axis=1)
                placed = jnp.where(at_top, rim, jnp.roll(placed, -1, axis=1))
            if step_y != 0:
                placed = jnp.roll(placed, step_y * depth_z, axis=1)
            shifted.append(placed)
        lattice = jnp.stack(shifted)
    final = lattice.reshape(Q, B, B, AVG, B).transpose(3, 0, 1, 2, 4)
    return final.reshape(AVG, Q, B * B * B)


def solution(mesh):
    return jax.shard_map(
        on_device,
        mesh=mesh,
        in_specs=(P(("grp", "dev"), None, None), P(("grp", "dev"), None), P("grp", None, None)),
        out_specs=P(("grp", "dev"), None, None),
        check_vma=False,
    )
```

profile of v0, /device:TPU:0, one launch (start us, length us, event | category | flops | bytes accessed | tf_op | source)
XLA Modules:
  0.0 258.2 jit_solution(3830552348423208224)
XLA Ops:
  5.5 3.4 %gather_fusion.10 = f32[2,19,4096]{2,0,1:T(2,128)S(1)} fusion(f32[4,19,4096]{2,0,1:T(4,128)} %param.17, s32[1024]{0:T(1024)S(1)} %get-tuple-element.276), kind=kCustom, calls=%fused_computation.1.clone | custom fusion | bytes 1245192 | tf_op jit(solution)/shard_map/jit(_take)/gather | solution.py:195
  10.1 6.2 %collective-permute-start.6 = (f32[2,19,4096]{2,0,1:T(2,128)}, f32[2,19,4096]{2,0,1:T(2,128)}, u32[]{:S(2)}, u32[]{:S(2)}) collective-permute-start(f32[2,19,4096]{2,0,1:T(2,128)} %broadcast_select_fusion.5), channel_id=1, source_target_pairs={{0,29},{1,30},{2,31},{3,0},{4,1},{5,2},{6,3},{7,4},{8,5},{9,6},{10... | collective-permute-start | bytes 1867784 | tf_op jit(solution)/shard_map/ppermute | solution.py:69
  28.3 2.9 %gather_fusion.11 = f32[2,19,4096]{2,0,1:T(2,128)S(1)} fusion(f32[4,19,4096]{2,0,1:T(4,128)S(1)} %copy-done.2, s32[1024]{0:T(1024)S(1)} %get-tuple-element.275), kind=kCustom, calls=%fused_computation.7.clone | custom fusion | bytes 1245192 | tf_op jit(solution)/shard_map/jit(_take)/gather | solution.py:195
  31.2 2.9 %gather_fusion.12 = f32[2,19,4096]{2,0,1:T(2,128)S(1)} fusion(f32[4,19,4096]{2,0,1:T(4,128)S(1)} %copy-done.2, s32[1024]{0:T(1024)S(1)} %get-tuple-element.274), kind=kCustom, calls=%fused_computation.8.clone | custom fusion | bytes 1245192 | tf_op jit(solution)/shard_map/jit(_take)/gather | solution.py:195
  34.2 2.9 %gather_fusion.13 = f32[2,19,4096]{2,0,1:T(2,128)S(1)} fusion(f32[4,19,4096]{2,0,1:T(4,128)S(1)} %copy-done.2, s32[1024]{0:T(1024)S(1)} %get-tuple-element.273), kind=kCustom, calls=%fused_computation.9.clone | custom fusion | bytes 1245192 | tf_op jit(solution)/shard_map/jit(_take)/gather | solution.py:195
  48.4 3.7 %gather_fusion.14 = f32[2,19,4096]{2,0,1:T(2,128)} fusion(f32[4,19,4096]{2,0,1:T(4,128)S(1)} %copy-done.2, s32[1024]{0:T(1024)S(1)} %get-tuple-element.272), kind=kCustom, calls=%fused_computation.10.clone | custom fusion | bytes 1245192 | tf_op jit(solution)/shard_map/jit(_take)/gather | solution.py:195
  52.7 3.8 %gather_fusion.15 = f32[2,19,4096]{2,0,1:T(2,128)} fusion(f32[4,19,4096]{2,0,1:T(4,128)S(1)} %copy-done.2, s32[1024]{0:T(1024)S(1)} %get-tuple-element.271), kind=kCustom, calls=%fused_computation.11.clone | custom fusion | bytes 1245192 | tf_op jit(solution)/shard_map/jit(_take)/gather | solution.py:195
  65.1 4.3 %collective-permute-start.7 = (f32[2,19,4096]{2,0,1:T(2,128)}, f32[2,19,4096]{2,0,1:T(2,128)}, u32[]{:S(2)}, u32[]{:S(2)}) collective-permute-start(f32[2,19,4096]{2,0,1:T(2,128)} %broadcast_select_fusion.4), channel_id=1, source_target_pairs={{0,30},{1,31},{2,0},{3,1},{4,2},{5,3},{6,4},{7,5},{8,6},{9,7},{10,... | collective-permute-start | bytes 1867784 | tf_op jit(solution)/shard_map/ppermute | solution.py:69
  75.1 10.1 %collective-permute-done.7 = f32[2,19,4096]{2,0,1:T(2,128)} collective-permute-done((f32[2,19,4096]{2,0,1:T(2,128)}, f32[2,19,4096]{2,0,1:T(2,128)}, u32[]{:S(2)}, u32[]{:S(2)}) %collective-permute-start.7) | collective-permute-done | bytes 622624 | tf_op jit(solution)/shard_map/ppermute | solution.py:69
  85.2 2.3 copy_dynamic-update-slice_fusion.5
  87.5 9.0 %collective-permute-done.8 = f32[2,19,4096]{2,0,1:T(2,128)} collective-permute-done((f32[2,19,4096]{2,0,1:T(2,128)S(1)}, f32[2,19,4096]{2,0,1:T(2,128)}, u32[]{:S(2)}, u32[]{:S(2)}) %collective-permute-start.8) | collective-permute-done | bytes 622624 | tf_op jit(solution)/shard_map/ppermute | solution.py:69
  101.2 2.3 copy_dynamic-update-slice_fusion.2
  103.5 3.3 %collective-permute-done.11 = f32[2,19,4096]{2,0,1:T(2,128)S(1)} collective-permute-done((f32[2,19,4096]{2,0,1:T(2,128)S(1)}, f32[2,19,4096]{2,0,1:T(2,128)S(1)}, u32[]{:S(2)}, u32[]{:S(2)}) %collective-permute-start.11) | collective-permute-done | bytes 622624 | tf_op jit(solution)/shard_map/ppermute | solution.py:69
  108.1 3.4 %gather_fusion.1 = f32[2,19,4096]{2,1,0:T(8,128)S(1)} fusion(f32[16,19,4096]{2,1,0:T(8,128)} %copy_dynamic-update-slice_fusion.1, s32[1024]{0:T(1024)S(1)} %pad_clamp_fusion.1), kind=kCustom, calls=%fused_computation.13 | custom fusion | bytes 1245192 | tf_op jit(solution)/shard_map/jit(_take)/gather | solution.py:202
  112.0 4.0 %gather.27 = f32[2,19,16,16,16]{4,3,2,0,1:T(8,128)} reshape(f32[2,19,4096]{2,0,1:T(2,128)S(1)} %copy.272) | data formatting | bytes 1245184 | tf_op jit(solution)/shard_map/jit(_take)/gather | solution.py:202
  116.0 2.9 %select_bitcast_fusion = f32[19,16,16,2,16]{4,2,1,3,0:T(8,128)S(1)} fusion(f32[2,19,16,16,16]{4,3,2,0,1:T(8,128)} %gather.27, pred[2]{0:T(512)(128)(4,1)S(1)} %compare_and_fusion.6), kind=kLoop, calls=%fused_computation.22 | loop fusion | flops 155648 | bytes 1245186 | tf_op jit(solution)/shard_map/transpose | solution.py:206
  120.2 6.1 %copy.273 = f32[19,16,16,2,16]{4,3,2,1,0:T(2,128)} copy(f32[19,16,16,2,16]{4,2,1,3,0:T(8,128)S(1)} %select_bitcast_fusion) | data formatting | bytes 1245184 | tf_op jit(solution)/shard_map/transpose | solution.py:206
  158.3 9.9 %reshape_reshape.3 = f32[19,8192]{1,0:T(8,128)S(1)} reshape(f32[19,16,16,2,16]{4,3,2,1,0:T(2,128)} %copy.273) | data formatting | bytes 1245184 | tf_op jit(solution)/shard_map/reshape;reshape | solution.py:212
  174.8 2.8 %collective-permute-start.13 = (f32[10,1,512]{2,1,0:T(1,128)S(1)}, f32[10,1,512]{2,1,0:T(1,128)S(1)}, u32[]{:S(2)}, u32[]{:S(2)}) collective-permute-start(f32[10,1,512]{2,1,0:T(1,128)S(1)} %get-tuple-element.202), channel_id=1, source_target_pairs={{32,0},{64,32},{96,64},{0,96},{33,1},{65,33},{97,65},{1,97},{34,2}... | collective-permute-start | bytes 61448 | tf_op jit(solution)/shard_map/ppermute | solution.py:81
  189.1 4.5 %collective-permute-done.14 = f32[5,16,16]{2,1,0:T(8,128)S(1)} collective-permute-done((f32[5,16,16]{2,1,0:T(8,128)S(1)}, f32[5,16,16]{2,1,0:T(8,128)S(1)}, u32[]{:S(2)}, u32[]{:S(2)}) %collective-permute-start.14) | collective-permute-done | bytes 5152 | tf_op jit(solution)/shard_map/ppermute | solution.py:69
  204.9 3.2 %collective-permute-start.17 = (f32[10,1,512]{2,1,0:T(1,128)S(1)}, f32[10,1,512]{2,1,0:T(1,128)S(1)}, u32[]{:S(2)}, u32[]{:S(2)}) collective-permute-start(f32[10,1,512]{2,1,0:T(1,128)S(1)} %get-tuple-element.199), channel_id=1, source_target_pairs={{32,0},{64,32},{96,64},{0,96},{33,1},{65,33},{97,65},{1,97},{34,2}... | collective-permute-start | bytes 61448 | tf_op jit(solution)/shard_map/ppermute | solution.py:81
  215.3 5.1 %collective-permute-start.19 = (f32[5,16,16]{2,1,0:T(8,128)S(1)}, f32[5,16,16]{2,1,0:T(8,128)S(1)}, u32[]{:S(2)}, u32[]{:S(2)}) collective-permute-start(f32[5,16,16]{2,1,0:T(8,128)S(1)} %constant_dynamic-update-slice_fusion.17), channel_id=1, source_target_pairs={{0,31},{1,0},{2,1},{3,2},{4,3},{5,4},{6,5},{7,6},{8,7},{9,8},{10,9... | collective-permute-start | bytes 15368 | tf_op jit(solution)/shard_map/ppermute | solution.py:69
  247.3 5.3 %copy.327 = f32[2,19,16,16,16]{4,3,2,0,1:T(8,128)} copy(f32[2,19,16,16,16]{4,0,3,2,1:T(2,128)} %bitcast.336) | data formatting | bytes 1245184 | tf_op jit(solution)/shard_map/transpose | solution.py:243
  252.6 5.3 %reshape.798 = f32[2,19,4096]{2,0,1:T(2,128)} reshape(f32[2,19,16,16,16]{4,3,2,0,1:T(8,128)} %copy.327) | data formatting | bytes 1245184 | tf_op jit(solution)/shard_map/reshape | solution.py:244
  (598 shorter events, 145.5 us)
Async XLA Ops:
  0.0 16.3 %copy-start.3 = (f32[4,4096]{1,0:T(4,128)S(1)}, f32[4,4096]{1,0:T(4,128)}, u32[]{:S(2)}) copy-start(f32[4,4096]{1,0:T(4,128)} %param.18) | copy-start | bytes 196612
  0.0 26.4 %copy-start.2 = (f32[4,19,4096]{2,0,1:T(4,128)S(1)}, f32[4,19,4096]{2,0,1:T(4,128)}, u32[]{:S(2)}) copy-start(f32[4,19,4096]{2,0,1:T(4,128)} %param.17) | copy-start | bytes 3735556
  10.1 62.3 %collective-permute-start.6 = (f32[2,19,4096]{2,0,1:T(2,128)}, f32[2,19,4096]{2,0,1:T(2,128)}, u32[]{:S(2)}, u32[]{:S(2)}) collective-permute-start(f32[2,19,4096]{2,0,1:T(2,128)} %broadcast_select_fusion.5), channel_id=1, source_target_pairs={{0,29},{1,30},{2,31},{3,0},{4,1},{5,2},{6,3},{7,4},{8,5},{9,6},{10... | collective-permute-start | bytes 1867784 | tf_op jit(solution)/shard_map/ppermute | solution.py:69
  17.0 44.3 %collective-permute-start = (f32[2,4096]{1,0:T(2,128)S(1)}, f32[2,4096]{1,0:T(2,128)S(1)}, u32[]{:S(2)}, u32[]{:S(2)}) collective-permute-start(f32[2,4096]{1,0:T(2,128)S(1)} %broadcast_select_fusion.11), channel_id=1, source_target_pairs={{0,29},{1,30},{2,31},{3,0},{4,1},{5,2},{6,3},{7,4},{8,5},{9,6},{10... | collective-permute-start | bytes 98312 | tf_op jit(solution)/shard_map/ppermute | solution.py:69
  18.5 43.6 %collective-permute-start.1 = (f32[2,4096]{1,0:T(2,128)S(1)}, f32[2,4096]{1,0:T(2,128)S(1)}, u32[]{:S(2)}, u32[]{:S(2)}) collective-permute-start(f32[2,4096]{1,0:T(2,128)S(1)} %broadcast_select_fusion.10), channel_id=1, source_target_pairs={{0,30},{1,31},{2,0},{3,1},{4,2},{5,3},{6,4},{7,5},{8,6},{9,7},{10,... | collective-permute-start | bytes 98312 | tf_op jit(solution)/shard_map/ppermute | solution.py:69
  24.0 41.2 %collective-permute-start.2 = (f32[2,4096]{1,0:T(2,128)S(1)}, f32[2,4096]{1,0:T(2,128)S(1)}, u32[]{:S(2)}, u32[]{:S(2)}) collective-permute-start(f32[2,4096]{1,0:T(2,128)S(1)} %broadcast_select_fusion.9), channel_id=1, source_target_pairs={{0,31},{1,0},{2,1},{3,2},{4,3},{5,4},{6,5},{7,6},{8,7},{9,8},{10,9... | collective-permute-start | bytes 98312 | tf_op jit(solution)/shard_map/ppermute | solution.py:69
  26.1 43.3 %collective-permute-start.3 = (f32[2,4096]{1,0:T(2,128)}, f32[2,4096]{1,0:T(2,128)S(1)}, u32[]{:S(2)}, u32[]{:S(2)}) collective-permute-start(f32[2,4096]{1,0:T(2,128)} %broadcast_select_fusion.8), channel_id=1, source_target_pairs={{0,1},{1,2},{2,3},{3,4},{4,5},{5,6},{6,7},{7,8},{8,9},{9,10},{10,1... | collective-permute-start | bytes 98312 | tf_op jit(solution)/shard_map/ppermute | solution.py:69
  57.1 131.9 %copy-start.19 = (pred[512]{0:T(512)(128)(4,1)}, pred[512]{0:T(512)(128)(4,1)S(1)}, u32[]{:S(2)}) copy-start(pred[512]{0:T(512)(128)(4,1)S(1)} %fusion.40) | copy-start | bytes 1540
  61.3 8.1 %collective-permute-start.4 = (f32[2,4096]{1,0:T(2,128)S(1)}, f32[2,4096]{1,0:T(2,128)S(1)}, u32[]{:S(2)}, u32[]{:S(2)}) collective-permute-start(f32[2,4096]{1,0:T(2,128)S(1)} %broadcast_select_fusion.7), channel_id=1, source_target_pairs={{0,2},{1,3},{2,4},{3,5},{4,6},{5,7},{6,8},{7,9},{8,10},{9,11},{10,... | collective-permute-start | bytes 98312 | tf_op jit(solution)/shard_map/ppermute | solution.py:69
  62.0 7.9 %collective-permute-start.5 = (f32[2,4096]{1,0:T(2,128)S(1)}, f32[2,4096]{1,0:T(2,128)S(1)}, u32[]{:S(2)}, u32[]{:S(2)}) collective-permute-start(f32[2,4096]{1,0:T(2,128)S(1)} %broadcast_select_fusion.6), channel_id=1, source_target_pairs={{0,3},{1,4},{2,5},{3,6},{4,7},{5,8},{6,9},{7,10},{8,11},{9,12},{10... | collective-permute-start | bytes 98312 | tf_op jit(solution)/shard_map/ppermute | solution.py:69
  65.1 20.1 %collective-permute-start.7 = (f32[2,19,4096]{2,0,1:T(2,128)}, f32[2,19,4096]{2,0,1:T(2,128)}, u32[]{:S(2)}, u32[]{:S(2)}) collective-permute-start(f32[2,19,4096]{2,0,1:T(2,128)} %broadcast_select_fusion.4), channel_id=1, source_target_pairs={{0,30},{1,31},{2,0},{3,1},{4,2},{5,3},{6,4},{7,5},{8,6},{9,7},{10,... | collective-permute-start | bytes 1867784 | tf_op jit(solution)/shard_map/ppermute | solution.py:69
  69.4 27.1 %collective-permute-start.8 = (f32[2,19,4096]{2,0,1:T(2,128)S(1)}, f32[2,19,4096]{2,0,1:T(2,128)}, u32[]{:S(2)}, u32[]{:S(2)}) collective-permute-start(f32[2,19,4096]{2,0,1:T(2,128)S(1)} %broadcast_select_fusion.3), channel_id=1, source_target_pairs={{0,31},{1,0},{2,1},{3,2},{4,3},{5,4},{6,5},{7,6},{8,7},{9,8},{10,9... | collective-permute-start | bytes 1867784 | tf_op jit(solution)/shard_map/ppermute | solution.py:69
  69.4 29.4 %collective-permute-start.9 = (f32[2,19,4096]{2,0,1:T(2,128)S(1)}, f32[2,19,4096]{2,0,1:T(2,128)}, u32[]{:S(2)}, u32[]{:S(2)}) collective-permute-start(f32[2,19,4096]{2,0,1:T(2,128)S(1)} %broadcast_select_fusion.2), channel_id=1, source_target_pairs={{0,1},{1,2},{2,3},{3,4},{4,5},{5,6},{6,7},{7,8},{8,9},{9,10},{10,1... | collective-permute-start | bytes 1867784 | tf_op jit(solution)/shard_map/ppermute | solution.py:69
  69.9 31.3 %collective-permute-start.10 = (f32[2,19,4096]{2,0,1:T(2,128)S(1)}, f32[2,19,4096]{2,0,1:T(2,128)}, u32[]{:S(2)}, u32[]{:S(2)}) collective-permute-start(f32[2,19,4096]{2,0,1:T(2,128)S(1)} %broadcast_select_fusion.1), channel_id=1, source_target_pairs={{0,2},{1,3},{2,4},{3,5},{4,6},{5,7},{6,8},{7,9},{8,10},{9,11},{10,... | collective-permute-start | bytes 1867784 | tf_op jit(solution)/shard_map/ppermute | solution.py:69
  72.5 34.3 %collective-permute-start.11 = (f32[2,19,4096]{2,0,1:T(2,128)S(1)}, f32[2,19,4096]{2,0,1:T(2,128)S(1)}, u32[]{:S(2)}, u32[]{:S(2)}) collective-permute-start(f32[2,19,4096]{2,0,1:T(2,128)S(1)} %broadcast_select_fusion), channel_id=1, source_target_pairs={{0,3},{1,4},{2,5},{3,6},{4,7},{5,8},{6,9},{7,10},{8,11},{9,12},{10... | collective-permute-start | bytes 1867784 | tf_op jit(solution)/shard_map/ppermute | solution.py:69
  174.8 8.0 %collective-permute-start.13 = (f32[10,1,512]{2,1,0:T(1,128)S(1)}, f32[10,1,512]{2,1,0:T(1,128)S(1)}, u32[]{:S(2)}, u32[]{:S(2)}) collective-permute-start(f32[10,1,512]{2,1,0:T(1,128)S(1)} %get-tuple-element.202), channel_id=1, source_target_pairs={{32,0},{64,32},{96,64},{0,96},{33,1},{65,33},{97,65},{1,97},{34,2}... | collective-permute-start | bytes 61448 | tf_op jit(solution)/shard_map/ppermute | solution.py:81
  177.6 5.0 %collective-permute-start.12 = (f32[10,1,512]{2,1,0:T(1,128)S(1)}, f32[10,1,512]{2,1,0:T(1,128)S(1)}, u32[]{:S(2)}, u32[]{:S(2)}) collective-permute-start(f32[10,1,512]{2,1,0:T(1,128)S(1)} %get-tuple-element.201), channel_id=1, source_target_pairs={{0,32},{32,64},{64,96},{96,0},{1,33},{33,65},{65,97},{97,1},{2,34}... | collective-permute-start | bytes 61448 | tf_op jit(solution)/shard_map/ppermute | solution.py:79
  184.2 4.3 %collective-permute-start.15 = (f32[5,16,16]{2,1,0:T(8,128)S(1)}, f32[5,16,16]{2,1,0:T(8,128)S(1)}, u32[]{:S(2)}, u32[]{:S(2)}) collective-permute-start(f32[5,16,16]{2,1,0:T(8,128)S(1)} %constant_dynamic-update-slice_fusion.6), channel_id=1, source_target_pairs={{0,31},{1,0},{2,1},{3,2},{4,3},{5,4},{6,5},{7,6},{8,7},{9,8},{10,9... | collective-permute-start | bytes 15368 | tf_op jit(solution)/shard_map/ppermute | solution.py:69
  186.7 7.0 %collective-permute-start.14 = (f32[5,16,16]{2,1,0:T(8,128)S(1)}, f32[5,16,16]{2,1,0:T(8,128)S(1)}, u32[]{:S(2)}, u32[]{:S(2)}) collective-permute-start(f32[5,16,16]{2,1,0:T(8,128)S(1)} %constant_dynamic-update-slice_fusion.1), channel_id=1, source_target_pairs={{0,1},{1,2},{2,3},{3,4},{4,5},{5,6},{6,7},{7,8},{8,9},{9,10},{10,1... | collective-permute-start | bytes 15368 | tf_op jit(solution)/shard_map/ppermute | solution.py:69
  204.9 7.8 %collective-permute-start.16 = (f32[10,1,512]{2,1,0:T(1,128)S(1)}, f32[10,1,512]{2,1,0:T(1,128)S(1)}, u32[]{:S(2)}, u32[]{:S(2)}) collective-permute-start(f32[10,1,512]{2,1,0:T(1,128)S(1)} %get-tuple-element.200), channel_id=1, source_target_pairs={{0,32},{32,64},{64,96},{96,0},{1,33},{33,65},{65,97},{97,1},{2,34}... | collective-permute-start | bytes 61448 | tf_op jit(solution)/shard_map/ppermute | solution.py:79
  204.9 7.4 %collective-permute-start.17 = (f32[10,1,512]{2,1,0:T(1,128)S(1)}, f32[10,1,512]{2,1,0:T(1,128)S(1)}, u32[]{:S(2)}, u32[]{:S(2)}) collective-permute-start(f32[10,1,512]{2,1,0:T(1,128)S(1)} %get-tuple-element.199), channel_id=1, source_target_pairs={{32,0},{64,32},{96,64},{0,96},{33,1},{65,33},{97,65},{1,97},{34,2}... | collective-permute-start | bytes 61448 | tf_op jit(solution)/shard_map/ppermute | solution.py:81
  211.9 15.8 %copy-start.20 = (pred[512]{0:T(512)(128)(4,1)S(1)}, pred[512]{0:T(512)(128)(4,1)}, u32[]{:S(2)}) copy-start(pred[512]{0:T(512)(128)(4,1)} %copy-done.19) | copy-start | bytes 1540
  214.8 13.1 %collective-permute-start.18 = (f32[5,16,16]{2,1,0:T(8,128)S(1)}, f32[5,16,16]{2,1,0:T(8,128)S(1)}, u32[]{:S(2)}, u32[]{:S(2)}) collective-permute-start(f32[5,16,16]{2,1,0:T(8,128)S(1)} %constant_dynamic-update-slice_fusion.12), channel_id=1, source_target_pairs={{0,1},{1,2},{2,3},{3,4},{4,5},{5,6},{6,7},{7,8},{8,9},{9,10},{10,1... | collective-permute-start | bytes 15368 | tf_op jit(solution)/shard_map/ppermute | solution.py:69
  215.3 11.9 %collective-permute-start.19 = (f32[5,16,16]{2,1,0:T(8,128)S(1)}, f32[5,16,16]{2,1,0:T(8,128)S(1)}, u32[]{:S(2)}, u32[]{:S(2)}) collective-permute-start(f32[5,16,16]{2,1,0:T(8,128)S(1)} %constant_dynamic-update-slice_fusion.17), channel_id=1, source_target_pairs={{0,31},{1,0},{2,1},{3,2},{4,3},{5,4},{6,5},{7,6},{8,7},{9,8},{10,9... | collective-permute-start | bytes 15368 | tf_op jit(solution)/shard_map/ppermute | solution.py:69
  (38 other events, 477.8 us)
where the time goes:
time: 263 us; the launch traced here: 258 us
  local copies, waits for them, and re-layouts  149 us (57%)
  other arithmetic  42.7 us (16%)
  starting transfers between devices  31.5 us (12%)
  waiting for transfers between devices  28.8 us (11%)
  matrix products  2.84 us (1%)
  between operations  2.8 us (1%)
    slice x39, local copies, waits for them, and re-layouts, collide(): reflected = jnp.stack([flat_cells[index] for index in mirror])  33 us
    unnamed x179, local copies, waits for them, and re-layouts  29.4 us
    ppermute x16, waiting for transfers between devices, shifted_2(): return lax.ppermute(value, axis, pairs)  27 us
    ppermute x16, starting transfers between devices, shifted_2(): return lax.ppermute(value, axis, pairs)  25.5 us
    gather x6, local copies, waits for them, and re-layouts, on_device(): jnp.take(populations, places, axis=0)  19.7 us
    sort x13, other arithmetic, ordered(): picked = jnp.sort(sort_keys)[:length]  13.2 us
    another operation x1, local copies, waits for them, and re-layouts, on_device(): lattice.reshape(Q, B * plane)  9.94 us
    unnamed x22, other arithmetic  8.96 us
  transfers between devices with their start and end apart: 20, of which 5 were waited for; matrix products, arithmetic and copies ran while one was open for 29% of the time, Pallas kernels for 0%

commit v1 on v0

v1 whole, which is shorter than its diff:
```python
import jax
import jax.numpy as jnp
import numpy as np
from jax import lax
from jax.experimental import pallas as pl
from jax.experimental.pallas import tpu as pltpu
from jax.sharding import PartitionSpec as P

MESH = pl.DeviceIdType.MESH
B = 16
AVG = 2
HS = 4
TEAM = 4
Q = 19
C = B * B * B
LANES = 128
TILES = C // LANES
CHUNKS = 2
PER_CHUNK = TILES // CHUNKS
CELL_ROWS = PER_CHUNK * Q
CHUNK_ROWS = CELL_ROWS + PER_CHUNK
MAIN = 8
ROWS = 32
NEXT_ROWS = 24

SPEEDS = [
    (0, 0, 0), (1, 0, 0), (-1, 0, 0), (0, 1, 0), (0, -1, 0), (0, 0, 1), (0, 0, -1), (1, 1, 0), (-1, -1, 0), (1, -1, 0),
    (-1, 1, 0), (1, 0, 1), (-1, 0, -1), (1, 0, -1), (-1, 0, 1), (0, 1, 1), (0, -1, -1), (0, 1, -1), (0, -1, 1),
]
SOLID = Q
ORDER = (
    [d for d in range(Q) if SPEEDS[d][0] == 1]
    + [SOLID]
    + [d for d in range(Q) if SPEEDS[d][0] == 0]
    + [d for d in range(Q) if SPEEDS[d][0] == -1]
)
SLOT = {d: place for place, d in enumerate(ORDER)}
SLOTS = Q + 1
FORWARD = 15

UP_FACE = [
    [(d, 15) for d in range(Q) if SPEEDS[d][2] >= 0] + [(SOLID, 15)],
    [(d, 14) for d in range(Q) if SPEEDS[d][2] == 1],
]
DOWN_FACE = [
    [(d, 0) for d in range(Q) if SPEEDS[d][2] <= 0] + [(SOLID, 0)],
    [(d, 1) for d in range(Q) if SPEEDS[d][2] == -1],
]


def rolled(value, amount):
    amount %= LANES
    return pltpu.roll(value, amount, 1) if amount else value


def collide(f, n):
    pair = {}
    gap = {}
    for i in range(1, Q, 2):
        pair[i] = f[i] + f[i + 1]
        gap[i] = f[i] - f[i + 1]
    xy, xz, yz = pair[7] + pair[9], pair[11] + pair[13], pair[15] + pair[17]
    axes_yz = pair[3] + pair[5]
    axes = pair[1] + axes_yz
    xy_xz = xy + xz
    diagonals = xy_xz + yz
    rho = f[0] + axes + diagonals
    energy = 8.0 * diagonals - 11.0 * axes - 30.0 * f[0]
    energy_2 = diagonals - 4.0 * axes + 12.0 * f[0]
    axial = 2.0 * pair[1] - axes_yz
    planar = xy_xz - 2.0 * yz
    axial_w = pair[3] - pair[5]
    planar_w = xy - xz
    gx_xy, gx_xz = gap[7] + gap[9], gap[11] + gap[13]
    gy_xy, gy_yz = gap[7] - gap[9], gap[15] + gap[17]
    gz_xz, gz_yz = gap[11] - gap[13], gap[15] - gap[17]
    dx, dy, dz = gx_xy + gx_xz, gy_xy + gy_yz, gz_xz + gz_yz
    jx, jy, jz = gap[1] + dx, gap[3] + dy, gap[5] + dz
    third = 1.0 / 3.0
    xx, yy, zz = jx * jx, jy * jy, jz * jz
    yyzz = yy + zz
    square = xx + yyzz
    p = (2.0 * third) * xx - third * yyzz
    w = third * (yy - zz)
    open_share = 1.0 - n

    def relaxed(rate, norm, excess):
        return (rate / norm) * excess

    r_e = open_share * relaxed(1.19, 2394.0, energy + 11.0 * rho - (19.0 * third) * square)
    r_e2 = open_share * relaxed(1.4, 252.0, energy_2 - 3.0 * rho + (5.5 * third) * square)
    r_p = open_share * relaxed(1.25, 36.0, axial + planar - p)
    r_p2 = open_share * relaxed(1.4, 72.0, planar - 2.0 * axial + 0.5 * p)
    r_w = open_share * relaxed(1.25, 12.0, axial_w + planar_w - w)
    r_w2 = open_share * relaxed(1.4, 24.0, planar_w - 2.0 * axial_w + 0.5 * w)
    third_j = (third * jx, third * jy)
    r_xy = open_share * relaxed(1.25, 4.0, pair[7] - pair[9] - third_j[0] * jy)
    r_yz = open_share * relaxed(1.25, 4.0, pair[15] - pair[17] - third_j[1] * jz)
    r_xz = open_share * relaxed(1.25, 4.0, pair[11] - pair[13] - third_j[0] * jz)
    r_qx = open_share * relaxed(1.2, 40.0, dx - 4.0 * gap[1] + (2.0 * third) * jx)
    r_qy = open_share * relaxed(1.2, 40.0, dy - 4.0 * gap[3] + (2.0 * third) * jy)
    r_qz = open_share * relaxed(1.2, 40.0, dz - 4.0 * gap[5] + (2.0 * third) * jz)
    r_mx = open_share * relaxed(1.98, 8.0, gx_xy - gx_xz)
    r_my = open_share * relaxed(1.98, 8.0, gy_yz - gy_xy)
    r_mz = open_share * relaxed(1.98, 8.0, gz_xz - gz_yz)

    even_axis = -11.0 * r_e - 4.0 * r_e2
    even_plane = 8.0 * r_e + r_e2
    a_p = r_p - 2.0 * r_p2
    a_w = r_w - 2.0 * r_w2
    d_p = r_p + r_p2
    d_w = r_w + r_w2
    axis_rest = even_axis - a_p
    plane_x = even_plane + d_p
    even_xy, even_xz, even_yz = plane_x + d_w, plane_x - d_w, even_plane - 2.0 * d_p
    x_plus, x_minus = r_qx + r_mx, r_qx - r_mx
    y_plus, y_minus = r_qy + r_my, r_qy - r_my
    z_plus, z_minus = r_qz + r_mz, r_qz - r_mz
    even = {
        1: even_axis + 2.0 * a_p,
        3: axis_rest + a_w,
        5: axis_rest - a_w,
        7: even_xy + r_xy,
        9: even_xy - r_xy,
        11: even_xz + r_xz,
        13: even_xz - r_xz,
        15: even_yz + r_yz,
        17: even_yz - r_yz,
    }
    odd = {
        1: -4.0 * r_qx,
        3: -4.0 * r_qy,
        5: -4.0 * r_qz,
        7: x_plus + y_minus,
        9: x_plus - y_minus,
        11: x_minus + z_plus,
        13: x_minus - z_plus,
        15: y_plus + z_minus,
        17: y_plus - z_minus,
    }
    post = [f[0] - (12.0 * r_e2 - 30.0 * r_e)]
    for i in range(1, Q, 2):
        turned = n * gap[i] + odd[i]
        post.append(f[i] - even[i] - turned)
        post.append(f[i + 1] - even[i] + turned)
    return post


def streamed(field, direction, block, half, row):
    step_x, step_y, step_z = SPEEDS[direction]
    lane = lax.broadcasted_iota(jnp.int32, (8, LANES), 1)

    def source(from_block):
        own = field[SLOT[direction], from_block, half, pl.ds(row - step_x, 8), :]
        if step_y == 0:
            return own
        other = field[SLOT[direction], from_block, 1 - half, pl.ds(row - step_x, 8), :]
        edge = lane >= LANES - B if step_y == 1 else lane < B
        return jnp.where(edge, other, own)

    inner = rolled(source(block), B * step_y + step_z)
    if step_z == 0:
        return inner
    beside = lax.rem(block + 3 - step_z, 3)
    outer = rolled(source(beside), B * step_y - (B - 1) * step_z)
    return jnp.where(lane % B == (0 if step_z == 1 else B - 1), outer, inner)


def kernel(
    populations, solidity, home_count, evolved,
    held, held_solid, *rest,
):
    pieces = CHUNKS * AVG
    sent, arrived = rest[:pieces], rest[pieces : 2 * pieces]
    (
        first, second, up_out, down_out, up_in, down_in, result,
        load_sem, move_send, move_recv, halo_send, halo_recv,
    ) = rest[2 * pieces :]
    n_grp, n_dev = lax.axis_size("grp"), lax.axis_size("dev")
    grp, dev = lax.axis_index("grp"), lax.axis_index("dev")
    before_g, after_g = lax.rem(grp + n_grp - 1, n_grp), lax.rem(grp + 1, n_grp)
    before_d, after_d = lax.rem(dev + n_dev - 1, n_dev), lax.rem(dev + 1, n_dev)
    member = lax.rem(dev, TEAM)
    team = lax.div(dev, TEAM)

    loads = [pltpu.make_async_copy(populations, held, load_sem.at[HS])] + [
        pltpu.make_async_copy(solidity.at[pl.ds(slot, 1)], held_solid.at[slot], load_sem.at[slot]) for slot in range(HS)
    ]
    for load in loads:
        load.start()
    around = [
        (grp, before_d), (grp, after_d), (before_g, dev), (after_g, dev),
        (before_g, before_d), (before_g, after_d), (after_g, before_d), (after_g, after_d),
    ]
    barrier = pltpu.get_barrier_semaphore()
    for device in around:
        pl.semaphore_signal(barrier, inc=1, device_id=device, device_id_type=MESH)

    counts = [home_count[0, team, j] for j in range(TEAM)]
    ends = []
    for j in range(TEAM):
        ends.append(counts[j] + (ends[-1] if ends else 0))
    start = jnp.int32(0)
    for j in range(1, TEAM):
        start = jnp.where(member == j, ends[j - 1], start)

    def local_slot(block):
        return jnp.clip(block - start, 0, HS - 1)

    def origin(block):
        holder = jnp.int32(0)
        for j in range(TEAM):
            holder = holder + (ends[j] <= block).astype(jnp.int32)
        return jnp.clip(holder - member + 1, 0, 2)

    for load in loads:
        load.wait()

    def stage(target, place, block, chunk):
        slot = local_slot(block)
        for k in range(PER_CHUNK):
            lanes = pl.ds((chunk * PER_CHUNK + k) * LANES, LANES)
            target[place, pl.ds(k * Q, 8), :] = held[slot, 0:8, lanes]
            target[place, pl.ds(k * Q + 8, 8), :] = held[slot, 8:16, lanes]
            target[place, pl.ds(k * Q + 16, 3), :] = held[slot, 16:19, lanes]
            target[place, pl.ds(CELL_ROWS + k, 1), :] = held_solid[slot, :, lanes]

    def to_before(piece):
        return pltpu.make_async_remote_copy(
            src_ref=sent[piece].at[0], dst_ref=arrived[piece].at[2], send_sem=move_send.at[0, piece],
            recv_sem=move_recv.at[0, piece], device_id=(grp, before_d), device_id_type=MESH,
        )

    def to_after(piece):
        return pltpu.make_async_remote_copy(
            src_ref=sent[piece].at[1], dst_ref=arrived[piece].at[0], send_sem=move_send.at[1, piece],
            recv_sem=move_recv.at[1, piece], device_id=(grp, after_d), device_id_type=MESH,
        )

    for piece in range(pieces):
        chunk, block = piece // AVG, piece % AVG
        stage(sent[piece], 0, AVG * (member - 1) + block, chunk)
        stage(sent[piece], 1, AVG * (member + 1) + block, chunk)
        if piece == 0:
            pl.semaphore_wait(barrier, len(around))

        @pl.when(member > 0)
        def _():
            to_before(piece).start()

        @pl.when(member < TEAM - 1)
        def _():
            to_after(piece).start()

    for piece in range(pieces):
        stage(arrived[piece], 1, AVG * member + piece % AVG, piece // AVG)

    for piece in range(pieces):
        chunk, block = piece // AVG, piece % AVG

        @pl.when(member > 0)
        def _():
            to_after(piece).wait_recv()

        @pl.when(member < TEAM - 1)
        def _():
            to_before(piece).wait_recv()

        where_from = origin(AVG * member + block)
        box = arrived[piece]
        for half in range(2):
            f = [box[where_from, pl.ds(half * Q + d, 8, stride=2 * Q), :] for d in range(Q)]
            n = box[where_from, pl.ds(CELL_ROWS + half, 8, stride=2), :]
            rows = pl.ds(MAIN + 8 * chunk, 8)
            for d, value in enumerate(collide(f, n) + [n]):
                first[SLOT[d], block, half, rows, :] = value

    def packed(face, block, half, row):
        lane = lax.broadcasted_iota(jnp.int32, (8, LANES), 1) % B
        out = []
        for items in face:
            total = None
            for place, (d, z) in enumerate(items):
                value = rolled(first[SLOT[d], block, half, pl.ds(row, 8), :], place - z)
                total = value if total is None else jnp.where(lane == place, value, total)
            out.append(total)
        return out

    def halo(index, source, target, device):
        return pltpu.make_async_remote_copy(
            src_ref=source, dst_ref=target, send_sem=halo_send.at[index], recv_sem=halo_recv.at[index],
            device_id=device, device_id_type=MESH,
        )

    low, high, body = pl.ds(MAIN - 2, 2), pl.ds(MAIN + B, 2), pl.ds(MAIN, B)
    top, bottom = pl.ds(MAIN + B - 2, 2), pl.ds(MAIN, 2)
    end, begin = pl.ds(B - 2, 2), pl.ds(0, 2)
    to_g, to_b = pl.ds(0, FORWARD), pl.ds(SLOTS - FORWARD, FORWARD)
    own = pl.ds(0, AVG)
    across = [
        halo(0, first.at[to_g, own, :, top, :], first.at[to_g, own, :, low, :], (after_g, dev)),
        halo(1, first.at[to_b, own, :, bottom, :], first.at[to_b, own, :, high, :], (before_g, dev)),
    ]
    along = [
        halo(2, up_out, up_in.at[:, :, body, :], (grp, after_d)),
        halo(3, up_out.at[:, :, end, :], up_in.at[:, :, low, :], (after_g, after_d)),
        halo(4, up_out.at[:, :, begin, :], up_in.at[:, :, high, :], (before_g, after_d)),
        halo(5, down_out, down_in.at[:, :, body, :], (grp, before_d)),
        halo(6, down_out.at[:, :, end, :], down_in.at[:, :, low, :], (after_g, before_d)),
        halo(7, down_out.at[:, :, begin, :], down_in.at[:, :, high, :], (before_g, before_d)),
    ]
    for copy in across:
        copy.start()
    for half in range(2):
        for part in range(2):
            for face, block, out in ((UP_FACE, AVG - 1, up_out), (DOWN_FACE, 0, down_out)):
                for place, value in enumerate(packed(face, block, half, MAIN + 8 * part)):
                    out[place, half, pl.ds(8 * part, 8), :] = value
    for copy in along:
        copy.start()
    for copy in across + along:
        copy.wait()

    lane = lax.broadcasted_iota(jnp.int32, (8, LANES), 1) % B
    faces = ((UP_FACE, up_in), (DOWN_FACE, down_in))

    @pl.loop(0, 8)
    def _(unit):
        half = lax.rem(unit, 2)
        rows = pl.ds(pl.multiple_of(lax.div(unit, 2) * 8, 8), 8)
        came = [[box[place, half, rows, :] for place in range(2)] for _, box in faces]
        for d in range(SLOTS):
            total = None
            for (face, _), vregs in zip(faces, came):
                for items, vreg in zip(face, vregs):
                    for place, (direction, z) in enumerate(items):
                        if direction == d:
                            value = rolled(vreg, z - place)
                            total = value if total is None else jnp.where(lane == z, value, total)
            first[SLOT[d], AVG, half, rows, :] = total

    @pl.loop(0, 6)
    def _(unit):
        block, half = lax.div(unit, 2), lax.rem(unit, 2)
        for part in range(NEXT_ROWS // 8):
            row = MAIN - 1 + 8 * part
            f = [streamed(first, d, block, half, row) for d in range(Q)]
            n = first[SLOT[SOLID], block, half, pl.ds(row, 8), :]
            for d, value in enumerate(collide(f, n)):
                second[SLOT[d], block, half, pl.ds(8 * part, 8), :] = value

    @pl.loop(0, 4)
    def _(unit):
        block, half = lax.div(unit, 2), lax.rem(unit, 2)
        for part in range(B // 8):
            for d in range(Q):
                value = streamed(second, d, block, half, 1 + 8 * part)
                result[block, pl.ds((16 * part + half) * Q + d, 8, stride=2 * Q), :] = value

    @pl.loop(0, AVG)
    def _(block):
        for k in range(TILES):
            lanes = pl.ds(k * LANES, LANES)
            evolved[block, 0:8, lanes] = result[block, pl.ds(k * Q, 8), :]
            evolved[block, 8:16, lanes] = result[block, pl.ds(k * Q + 8, 8), :]
            evolved[block, 16:19, lanes] = result[block, pl.ds(k * Q + 16, 3), :]

    for piece in range(pieces):
        @pl.when(member > 0)
        def _():
            to_before(piece).wait_send()

        @pl.when(member < TEAM - 1)
        def _():
            to_after(piece).wait_send()


def on_device(populations, solidity, home_count):
    pieces = CHUNKS * AVG
    f32 = jnp.float32
    return pl.pallas_call(
        kernel,
        out_shape=jax.ShapeDtypeStruct((AVG, Q, C), f32),
        in_specs=[
            pl.BlockSpec(memory_space=pl.ANY),
            pl.BlockSpec(memory_space=pl.ANY),
            pl.BlockSpec(memory_space=pltpu.SMEM),
        ],
        out_specs=pl.BlockSpec(memory_space=pltpu.VMEM),
        scratch_shapes=[
            pltpu.VMEM((HS, Q, C), f32),
            pltpu.VMEM((HS, 1, C), f32),
            *[pltpu.VMEM((2, CHUNK_ROWS, LANES), f32) for _ in range(pieces)],
            *[pltpu.VMEM((3, CHUNK_ROWS, LANES), f32) for _ in range(pieces)],
            pltpu.VMEM((SLOTS, AVG + 1, 2, ROWS, LANES), f32),
            pltpu.VMEM((SLOTS, AVG + 1, 2, NEXT_ROWS, LANES), f32),
            pltpu.VMEM((2, 2, B, LANES), f32),
            pltpu.VMEM((2, 2, B, LANES), f32),
            pltpu.VMEM((2, 2, ROWS, LANES), f32),
            pltpu.VMEM((2, 2, ROWS, LANES), f32),
            pltpu.VMEM((AVG, TILES * Q, LANES), f32),
            pltpu.SemaphoreType.DMA((HS + 1,)),
            pltpu.SemaphoreType.DMA((2, pieces)),
            pltpu.SemaphoreType.DMA((2, pieces)),
            pltpu.SemaphoreType.DMA((8,)),
            pltpu.SemaphoreType.DMA((8,)),
        ],
        compiler_params=pltpu.CompilerParams(
            collective_id=0, has_side_effects=True, vmem_limit_bytes=48 * 1024 * 1024
        ),
        cost_estimate=pl.CostEstimate(flops=8_000_000, bytes_accessed=3_000_000, transcendentals=0),
    )(populations, solidity, home_count)


def solution(mesh):
    return jax.shard_map(
        on_device,
        mesh=mesh,
        in_specs=(P(("grp", "dev"), None, None), P(("grp", "dev"), None), P("grp", None, None)),
        out_specs=P(("grp", "dev"), None, None),
        check_vma=False,
    )
```

time: 263 us -> 25.4 us (0.10)
  the two profiles are of different devices: /device:TPU:0 before, /device:TPU:1 now
where the time goes in v1:
time: 25.4 us; the launch traced here: 25.2 us
  Pallas kernels  21.1 us (83%)
  local copies, waits for them, and re-layouts  4.12 us (16%)
    pallas_call x1, Pallas kernels, on_device(): pl.pallas_call(kernel, out_shape=jax.ShapeDtypeStruct((AVG, Q, C), f32),...  21.1 us
    unnamed x4, local copies, waits for them, and re-layouts  2.81 us
    pallas_call x1, local copies, waits for them, and re-layouts, on_device(): pl.pallas_call(kernel, out_shape=jax.ShapeDtypeStruct((AVG, Q, C), f32),...  1.31 us

profile of v1, /device:TPU:1, one launch (start us, length us, event | category | flops | bytes accessed | tf_op | source)
XLA Modules:
  0.0 25.2 jit_solution(16438025025385728542)
XLA Ops:
  0.0 0.0 copy-start
  0.0 0.8 %copy.5.home_count = s32[1,8,4]{2,1,0:T(8,128)S(1)} copy(s32[1,8,4]{1,2,0:T(4,128)} %param.5) | data formatting | bytes 256 | tf_op args[2]
  0.8 2.0 %copy.4.populations = f32[4,19,4096]{2,1,0:T(8,128)S(1)} copy(f32[4,19,4096]{2,0,1:T(4,128)} %param.3) | data formatting | bytes 2490368 | tf_op args[0]
  2.8 0.0 copy-done
  2.8 21.1 %shard_map.37 = f32[2,19,4096]{2,1,0:T(8,128)S(1)} custom-call(f32[4,19,4096]{2,1,0:T(8,128)S(1)} %copy.4.populations, f32[4,4096]{1,0:T(4,128)S(1)} %copy-done, s32[1,8,4]{2,1,0:T(8,128)S(1)} %copy.5.home_count), custom_call_target="tpu_custom_call" | custom-call | flops 8000000 | bytes 3000000 | tf_op jit(solution)/shard_map/pallas_call | solution.py:381
  23.9 1.3 %copy.6 = f32[2,19,4096]{2,0,1:T(2,128)} copy(f32[2,19,4096]{2,1,0:T(8,128)S(1)} %shard_map.37) | data formatting | bytes 1245184 | tf_op jit(solution)/shard_map/pallas_call | solution.py:381
Async XLA Ops:
  0.0 2.8 %copy-start = (f32[4,4096]{1,0:T(4,128)S(1)}, f32[4,4096]{1,0:T(4,128)}, u32[]{:S(2)}) copy-start(f32[4,4096]{1,0:T(4,128)} %solidity.1) | copy-start | bytes 196612

commit v2 on v1

v2 whole, which is shorter than its diff:
```python
import jax
import jax.numpy as jnp
import numpy as np
from jax import lax
from jax.experimental import pallas as pl
from jax.experimental.pallas import tpu as pltpu
from jax.sharding import PartitionSpec as P

MESH = pl.DeviceIdType.MESH
B = 16
AVG = 2
HS = 4
TEAM = 4
Q = 19
C = B * B * B
LANES = 128
TILES = C // LANES
SOLID = Q
FIELDS = Q + 1
HALVES = 2
MAIN = 8
ROWS = 32
NEXT_ROWS = 24
OUTER = [(0, 5), (11, 5)]
INNER = [(5, 6)]
CHUNKS = [OUTER, INNER]
DEPTH = [sum(size for _, size in spans) for spans in CHUNKS]

SPEEDS = [
    (0, 0, 0), (1, 0, 0), (-1, 0, 0), (0, 1, 0), (0, -1, 0), (0, 0, 1), (0, 0, -1), (1, 1, 0), (-1, -1, 0), (1, -1, 0),
    (-1, 1, 0), (1, 0, 1), (-1, 0, -1), (1, 0, -1), (-1, 0, 1), (0, 1, 1), (0, -1, -1), (0, 1, -1), (0, -1, 1),
]
ORDER = (
    [d for d in range(Q) if SPEEDS[d][0] == 1]
    + [SOLID]
    + [d for d in range(Q) if SPEEDS[d][0] == 0]
    + [d for d in range(Q) if SPEEDS[d][0] == -1]
)
SLOT = {d: place for place, d in enumerate(ORDER)}
FORWARD = 15

UP_FACE = [
    [(d, 15) for d in range(Q) if SPEEDS[d][2] >= 0] + [(SOLID, 15)],
    [(d, 14) for d in range(Q) if SPEEDS[d][2] == 1],
]
DOWN_FACE = [
    [(d, 0) for d in range(Q) if SPEEDS[d][2] <= 0] + [(SOLID, 0)],
    [(d, 1) for d in range(Q) if SPEEDS[d][2] == -1],
]


def rolled(value, amount):
    amount %= LANES
    return pltpu.roll(value, amount, 1) if amount else value


def collide(f, n):
    pair = {}
    gap = {}
    for i in range(1, Q, 2):
        pair[i] = f[i] + f[i + 1]
        gap[i] = f[i] - f[i + 1]
    xy, xz, yz = pair[7] + pair[9], pair[11] + pair[13], pair[15] + pair[17]
    axes_yz = pair[3] + pair[5]
    axes = pair[1] + axes_yz
    xy_xz = xy + xz
    diagonals = xy_xz + yz
    rho = f[0] + axes + diagonals
    energy = 8.0 * diagonals - 11.0 * axes - 30.0 * f[0]
    energy_2 = diagonals - 4.0 * axes + 12.0 * f[0]
    axial = 2.0 * pair[1] - axes_yz
    planar = xy_xz - 2.0 * yz
    axial_w = pair[3] - pair[5]
    planar_w = xy - xz
    gx_xy, gx_xz = gap[7] + gap[9], gap[11] + gap[13]
    gy_xy, gy_yz = gap[7] - gap[9], gap[15] + gap[17]
    gz_xz, gz_yz = gap[11] - gap[13], gap[15] - gap[17]
    dx, dy, dz = gx_xy + gx_xz, gy_xy + gy_yz, gz_xz + gz_yz
    jx, jy, jz = gap[1] + dx, gap[3] + dy, gap[5] + dz
    third = 1.0 / 3.0
    xx, yy, zz = jx * jx, jy * jy, jz * jz
    yyzz = yy + zz
    square = xx + yyzz
    p = (2.0 * third) * xx - third * yyzz
    w = third * (yy - zz)
    open_share = 1.0 - n

    def relaxed(rate, norm, excess):
        return (rate / norm) * excess

    r_e = open_share * relaxed(1.19, 2394.0, energy + 11.0 * rho - (19.0 * third) * square)
    r_e2 = open_share * relaxed(1.4, 252.0, energy_2 - 3.0 * rho + (5.5 * third) * square)
    r_p = open_share * relaxed(1.25, 36.0, axial + planar - p)
    r_p2 = open_share * relaxed(1.4, 72.0, planar - 2.0 * axial + 0.5 * p)
    r_w = open_share * relaxed(1.25, 12.0, axial_w + planar_w - w)
    r_w2 = open_share * relaxed(1.4, 24.0, planar_w - 2.0 * axial_w + 0.5 * w)
    third_j = (third * jx, third * jy)
    r_xy = open_share * relaxed(1.25, 4.0, pair[7] - pair[9] - third_j[0] * jy)
    r_yz = open_share * relaxed(1.25, 4.0, pair[15] - pair[17] - third_j[1] * jz)
    r_xz = open_share * relaxed(1.25, 4.0, pair[11] - pair[13] - third_j[0] * jz)
    r_qx = open_share * relaxed(1.2, 40.0, dx - 4.0 * gap[1] + (2.0 * third) * jx)
    r_qy = open_share * relaxed(1.2, 40.0, dy - 4.0 * gap[3] + (2.0 * third) * jy)
    r_qz = open_share * relaxed(1.2, 40.0, dz - 4.0 * gap[5] + (2.0 * third) * jz)
    r_mx = open_share * relaxed(1.98, 8.0, gx_xy - gx_xz)
    r_my = open_share * relaxed(1.98, 8.0, gy_yz - gy_xy)
    r_mz = open_share * relaxed(1.98, 8.0, gz_xz - gz_yz)

    even_axis = -11.0 * r_e - 4.0 * r_e2
    even_plane = 8.0 * r_e + r_e2
    a_p = r_p - 2.0 * r_p2
    a_w = r_w - 2.0 * r_w2
    d_p = r_p + r_p2
    d_w = r_w + r_w2
    axis_rest = even_axis - a_p
    plane_x = even_plane + d_p
    even_xy, even_xz, even_yz = plane_x + d_w, plane_x - d_w, even_plane - 2.0 * d_p
    x_plus, x_minus = r_qx + r_mx, r_qx - r_mx
    y_plus, y_minus = r_qy + r_my, r_qy - r_my
    z_plus, z_minus = r_qz + r_mz, r_qz - r_mz
    even = {
        1: even_axis + 2.0 * a_p,
        3: axis_rest + a_w,
        5: axis_rest - a_w,
        7: even_xy + r_xy,
        9: even_xy - r_xy,
        11: even_xz + r_xz,
        13: even_xz - r_xz,
        15: even_yz + r_yz,
        17: even_yz - r_yz,
    }
    odd = {
        1: -4.0 * r_qx,
        3: -4.0 * r_qy,
        5: -4.0 * r_qz,
        7: x_plus + y_minus,
        9: x_plus - y_minus,
        11: x_minus + z_plus,
        13: x_minus - z_plus,
        15: y_plus + z_minus,
        17: y_plus - z_minus,
    }
    post = [f[0] - (12.0 * r_e2 - 30.0 * r_e)]
    for i in range(1, Q, 2):
        turned = n * gap[i] + odd[i]
        post.append(f[i] - even[i] - turned)
        post.append(f[i + 1] - even[i] + turned)
    return post


def streamed(field, direction, block, half, row, size):
    step_x, step_y, step_z = SPEEDS[direction]
    lane = lax.broadcasted_iota(jnp.int32, (size, LANES), 1)

    def source(from_block):
        own = field[SLOT[direction], from_block, half, pl.ds(row - step_x, size), :]
        if step_y == 0:
            return own
        other = field[SLOT[direction], from_block, 1 - half, pl.ds(row - step_x, size), :]
        edge = lane >= LANES - B if step_y == 1 else lane < B
        return jnp.where(edge, other, own)

    inner = rolled(source(block), B * step_y + step_z)
    if step_z == 0:
        return inner
    beside = lax.rem(block + 3 - step_z, 3)
    outer = rolled(source(beside), B * step_y - (B - 1) * step_z)
    return jnp.where(lane % B == (0 if step_z == 1 else B - 1), outer, inner)


def kernel(populations, solidity, home_count, evolved, held, counted, *rest):
    pieces = [(chunk, block) for chunk in range(len(CHUNKS)) for block in range(AVG)]
    sent, arrived = rest[: len(pieces)], rest[len(pieces) : 2 * len(pieces)]
    (
        first, second, up_outer, up_inner, down_outer, down_inner, up_outer_in, up_inner_in, up_corner_in,
        down_outer_in, down_inner_in, down_corner_in, load_sem, move_send, move_recv, halo_send, halo_recv,
    ) = rest[2 * len(pieces) :]
    n_grp, n_dev = lax.axis_size("grp"), lax.axis_size("dev")
    grp, dev = lax.axis_index("grp"), lax.axis_index("dev")
    before_g, after_g = lax.rem(grp + n_grp - 1, n_grp), lax.rem(grp + 1, n_grp)
    before_d, after_d = lax.rem(dev + n_dev - 1, n_dev), lax.rem(dev + 1, n_dev)
    member = lax.rem(dev, TEAM)
    team = lax.div(dev, TEAM)

    loads = [
        pltpu.make_async_copy(home_count, counted, load_sem.at[0]),
        pltpu.make_async_copy(populations, held.at[pl.ds(0, Q * TILES * HS)], load_sem.at[1]),
        pltpu.make_async_copy(solidity, held.at[pl.ds(Q * TILES * HS, TILES * HS)], load_sem.at[2]),
    ]
    for load in loads:
        load.start()
    around = [
        (grp, before_d), (grp, after_d), (before_g, dev), (after_g, dev),
        (before_g, before_d), (before_g, after_d), (after_g, before_d), (after_g, after_d),
    ]
    barrier = pltpu.get_barrier_semaphore()
    for device in around:
        pl.semaphore_signal(barrier, inc=1, device_id=device, device_id_type=MESH)
    for load in loads:
        load.wait()

    ends = []
    for j in range(TEAM):
        ends.append(counted[0, j, team] + (ends[-1] if ends else 0))
    start = jnp.int32(0)
    for j in range(1, TEAM):
        start = jnp.where(member == j, ends[j - 1], start)

    def origin(block):
        holder = jnp.int32(0)
        for j in range(TEAM):
            holder = holder + (ends[j] <= block).astype(jnp.int32)
        return jnp.clip(holder - member + 1, 0, 2)

    def stage(target, place, block, chunk):
        slot = jnp.clip(block - start, 0, HS - 1)
        stride = HS * HALVES
        for half in range(HALVES):
            for field in range(FIELDS):
                to = field * DEPTH[chunk]
                for x, size in CHUNKS[chunk]:
                    at = (field * TILES + HALVES * x + half) * HS
                    target[place, half, pl.ds(to, size), :] = held[pl.ds(at + slot, size, stride=stride), :]
                    to += size

    def to_before(piece):
        return pltpu.make_async_remote_copy(
            src_ref=sent[piece].at[0], dst_ref=arrived[piece].at[2], send_sem=move_send.at[0, piece],
            recv_sem=move_recv.at[0, piece], device_id=(grp, before_d), device_id_type=MESH,
        )

    def to_after(piece):
        return pltpu.make_async_remote_copy(
            src_ref=sent[piece].at[1], dst_ref=arrived[piece].at[0], send_sem=move_send.at[1, piece],
            recv_sem=move_recv.at[1, piece], device_id=(grp, after_d), device_id_type=MESH,
        )

    for piece, (chunk, block) in enumerate(pieces):
        stage(sent[piece], 0, AVG * (member - 1) + block, chunk)
        stage(sent[piece], 1, AVG * (member + 1) + block, chunk)
        if piece == 0:
            pl.semaphore_wait(barrier, len(around))

        @pl.when(member > 0)
        def _():
            to_before(piece).start()

        @pl.when(member < TEAM - 1)
        def _():
            to_after(piece).start()

    for piece, (chunk, block) in enumerate(pieces):
        stage(arrived[piece], 1, AVG * member + block, chunk)

    def settle(piece):
        chunk, block = pieces[piece]

        @pl.when(member > 0)
        def _():
            to_after(piece).wait_recv()

        @pl.when(member < TEAM - 1)
        def _():
            to_before(piece).wait_recv()

        place = origin(AVG * member + block)
        box = arrived[piece]
        for half in range(HALVES):
            begin = 0
            for x, size in CHUNKS[chunk]:
                f = [box[place, half, pl.ds(d * DEPTH[chunk] + begin, size), :] for d in range(FIELDS)]
                for d, value in enumerate(collide(f[:Q], f[SOLID]) + f[Q:]):
                    first[SLOT[d], block, half, pl.ds(MAIN + x, size), :] = value
                begin += size

    def pack(face, block, spans, target):
        for half in range(HALVES):
            for part, (x, size) in enumerate(spans):
                lane = lax.broadcasted_iota(jnp.int32, (size, LANES), 1) % B
                for place, items in enumerate(face):
                    total = None
                    for slot, (d, z) in enumerate(items):
                        value = rolled(first[SLOT[d], block, half, pl.ds(MAIN + x, size), :], slot - z)
                        total = value if total is None else jnp.where(lane == slot, value, total)
                    target[place, half, pl.ds(8 * part, size), :] = total

    def unpack(up, down, spans):
        for part, (begin, x, size) in enumerate(spans):
            lane = lax.broadcasted_iota(jnp.int32, (size, LANES), 1) % B

            @pl.loop(0, HALVES)
            def _(half):
                came = [[box[place, half, pl.ds(begin, size), :] for place in range(2)] for box in (up, down)]
                for d in range(FIELDS):
                    total = None
                    for face, vregs in zip((UP_FACE, DOWN_FACE), came):
                        for items, vreg in zip(face, vregs):
                            for slot, (direction, z) in enumerate(items):
                                if direction == d:
                                    value = rolled(vreg, z - slot)
                                    total = value if total is None else jnp.where(lane == z, value, total)
                    first[SLOT[d], AVG, half, pl.ds(MAIN + x, size), :] = total

    def halo(index, source, target, device):
        return pltpu.make_async_remote_copy(
            src_ref=source, dst_ref=target, send_sem=halo_send.at[index], recv_sem=halo_recv.at[index],
            device_id=device, device_id_type=MESH,
        )

    low, high = pl.ds(MAIN - 2, 2), pl.ds(MAIN + B, 2)
    top, bottom = pl.ds(MAIN + B - 2, 2), pl.ds(MAIN, 2)
    end, begin = pl.ds(8 + OUTER[1][1] - 2, 2), pl.ds(0, 2)
    to_g, to_b = pl.ds(0, FORWARD), pl.ds(FIELDS - FORWARD, FORWARD)
    own = pl.ds(0, AVG)
    across = [
        halo(0, first.at[to_g, own, :, top, :], first.at[to_g, own, :, low, :], (after_g, dev)),
        halo(1, first.at[to_b, own, :, bottom, :], first.at[to_b, own, :, high, :], (before_g, dev)),
    ]
    outer = [
        halo(2, up_outer, up_outer_in, (grp, after_d)),
        halo(3, down_outer, down_outer_in, (grp, before_d)),
        halo(4, up_outer.at[:, :, end, :], up_corner_in.at[:, :, pl.ds(0, 2), :], (after_g, after_d)),
        halo(5, up_outer.at[:, :, begin, :], up_corner_in.at[:, :, pl.ds(2, 2), :], (before_g, after_d)),
        halo(6, down_outer.at[:, :, end, :], down_corner_in.at[:, :, pl.ds(0, 2), :], (after_g, before_d)),
        halo(7, down_outer.at[:, :, begin, :], down_corner_in.at[:, :, pl.ds(2, 2), :], (before_g, before_d)),
    ]
    inner = [
        halo(8, up_inner, up_inner_in, (grp, after_d)),
        halo(9, down_inner, down_inner_in, (grp, before_d)),
    ]

    def step(spans):
        def once(block, half, x, size, keep):
            f = [streamed(first, d, block, half, MAIN + x, size) for d in range(Q)]
            n = first[SLOT[SOLID], block, half, pl.ds(MAIN + x, size), :]
            for d, value in enumerate(collide(f, n)):
                if d in keep:
                    second[SLOT[d], block, half, pl.ds(x + 1, size), :] = value

        @pl.loop(0, AVG * HALVES)
        def _(unit):
            for x, size in spans:
                once(lax.div(unit, 2), lax.rem(unit, 2), x, size, range(Q))

        @pl.loop(0, HALVES)
        def _(half):
            for x, size in spans:
                once(AVG, half, x, size, [d for d in range(Q) if SPEEDS[d][2]])

    settle(0)
    settle(1)
    for copy in across:
        copy.start()
    pack(UP_FACE, AVG - 1, OUTER, up_outer)
    pack(DOWN_FACE, 0, OUTER, down_outer)
    for copy in outer:
        copy.start()
    settle(2)
    settle(3)
    pack(UP_FACE, AVG - 1, INNER, up_inner)
    pack(DOWN_FACE, 0, INNER, down_inner)
    for copy in inner:
        copy.start()
    for copy in across + outer:
        copy.wait()
    unpack(up_outer_in, down_outer_in, [(0, 0, 5), (8, 11, 5)])
    unpack(up_corner_in, down_corner_in, [(0, -2, 2), (2, B, 2)])
    step([(-1, 5), (12, 5)])
    for copy in inner:
        copy.wait()
    unpack(up_inner_in, down_inner_in, [(0, 5, 6)])
    step([(4, 8)])

    for block in range(AVG):
        for half in range(HALVES):
            for x in range(0, B, 8):
                for d in range(Q):
                    at = (d * TILES + HALVES * x + half) * AVG + block
                    evolved[pl.ds(at, 8, stride=AVG * HALVES), :] = streamed(second, d, block, half, x + 1, 8)

    for piece in range(len(pieces)):
        @pl.when(member > 0)
        def _():
            to_before(piece).wait_send()

        @pl.when(member < TEAM - 1)
        def _():
            to_after(piece).wait_send()


def on_device(populations, solidity, home_count):
    f32 = jnp.float32
    populations = populations.transpose(1, 0, 2).reshape(Q, HS, TILES, LANES).transpose(0, 2, 1, 3).reshape(-1, LANES)
    solidity = solidity.reshape(HS, TILES, LANES).transpose(1, 0, 2).reshape(-1, LANES)
    home_count = home_count.transpose(0, 2, 1)
    arguments = [pltpu.with_memory_space_constraint(a, pltpu.HBM) for a in (populations, solidity, home_count)]

    def boxes(places):
        return [pltpu.VMEM((places, HALVES, FIELDS * depth, LANES), f32) for depth in DEPTH for _ in range(AVG)]

    def faces():
        return [pltpu.VMEM((2, HALVES, 16, LANES), f32), pltpu.VMEM((2, HALVES, 8, LANES), f32)]

    copies = len(CHUNKS) * AVG
    evolved = pl.pallas_call(
        kernel,
        out_shape=jax.ShapeDtypeStruct((Q * TILES * AVG, LANES), f32),
        in_specs=[pl.BlockSpec(memory_space=pltpu.HBM)] * 3,
        out_specs=pl.BlockSpec(memory_space=pltpu.VMEM),
        scratch_shapes=[
            pltpu.VMEM((FIELDS * TILES * HS, LANES), f32),
            pltpu.SMEM(home_count.shape, jnp.int32),
            *boxes(2),
            *boxes(3),
            pltpu.VMEM((FIELDS, AVG + 1, HALVES, ROWS, LANES), f32),
            pltpu.VMEM((FIELDS, AVG + 1, HALVES, NEXT_ROWS, LANES), f32),
            *faces(),
            *faces(),
            *faces(),
            pltpu.VMEM((2, HALVES, 8, LANES), f32),
            *faces(),
            pltpu.VMEM((2, HALVES, 8, LANES), f32),
            pltpu.SemaphoreType.DMA((3,)),
            pltpu.SemaphoreType.DMA((2, copies)),
            pltpu.SemaphoreType.DMA((2, copies)),
            pltpu.SemaphoreType.DMA((10,)),
            pltpu.SemaphoreType.DMA((10,)),
        ],
        compiler_params=pltpu.CompilerParams(
            collective_id=0, has_side_effects=True, vmem_limit_bytes=48 * 1024 * 1024
        ),
        cost_estimate=pl.CostEstimate(flops=8_000_000, bytes_accessed=3_000_000, transcendentals=0),
    )(*arguments)
    return evolved.reshape(Q, TILES, AVG, LANES).transpose(2, 0, 1, 3).reshape(AVG, Q, C)


def solution(mesh):
    return jax.shard_map(
        on_device,
        mesh=mesh,
        in_specs=(P(("grp", "dev"), None, None), P(("grp", "dev"), None), P("grp", None, None)),
        out_specs=P(("grp", "dev"), None, None),
        check_vma=False,
    )
```

time: 25.4 us -> 19.1 us (0.75)
  local copies, waits for them, and re-layouts: 4.12 us -> 0.83 us
  Pallas kernels: 21.1 us -> 18.2 us
    pallas_call x1, Pallas kernels: 21.1 us -> 18.2 us  [on_device(): pl.pallas_call(kernel, out_shape=jax.ShapeDtypeStruct((Q * TILES * AVG, L...]
    unnamed x4 -> x1, local copies, waits for them, and re-layouts: 2.81 us -> 0.83 us
    pallas_call x1 -> x0, local copies, waits for them, and re-layouts: 1.31 us -> none  [on_device(): pl.pallas_call(kernel, out_shape=jax.ShapeDtypeStruct((AVG, Q, C), f32),...]
where the time goes in v2:
time: 19.1 us; the launch traced here: 19 us
  Pallas kernels  18.2 us (95%)
  local copies, waits for them, and re-layouts  0.83 us (4%)
    pallas_call x1, Pallas kernels, on_device(): pl.pallas_call(kernel, out_shape=jax.ShapeDtypeStruct((Q * TILES * AVG, L...  18.2 us
    unnamed x1, local copies, waits for them, and re-layouts  0.83 us

profile of v2, /device:TPU:1, one launch (start us, length us, event | category | flops | bytes accessed | tf_op | source)
XLA Modules:
  0.0 19.0 jit_solution(498630004766566551)
XLA Ops:
  0.0 18.2 %shard_map.37 = f32[1216,128]{1,0:T(8,128)S(1)} custom-call(f32[2432,128]{1,0:T(8,128)} %bitcast.19, f32[128,128]{1,0:T(8,128)} %bitcast.20, s32[1,4,8]{2,1,0:T(4,128)} %bitcast.21), custom_call_target="tpu_custom_call" | custom-call | flops 8000000 | bytes 3000000 | tf_op jit(solution)/shard_map/pallas_call | solution.py:404
  18.2 0.8 %copy.8 = f32[2,19,4096]{2,0,1:T(2,128)} copy(f32[2,19,4096]{2,0,1:T(2,128)S(1)} %bitcast.18) | data formatting | bytes 1245184

commit v3 on v2

v3 whole, which is shorter than its diff:
```python
import jax
import jax.numpy as jnp
import numpy as np
from jax import lax
from jax.experimental import pallas as pl
from jax.experimental.pallas import tpu as pltpu
from jax.sharding import PartitionSpec as P

MESH = pl.DeviceIdType.MESH
B = 16
AVG = 2
HS = 4
TEAM = 4
Q = 19
C = B * B * B
LANES = 128
TILES = C // LANES
SOLID = Q
FIELDS = Q + 1
HALVES = 2
MAIN = 8
ROWS = 32
NEXT_ROWS = 24
OUTER = [[(half, x, 2) for half in range(HALVES) for x in (0, 14)]]
MIDDLE = [[(half, 2, 4), (half, 10, 4)] for half in range(HALVES)]
CORE = [[(half, 6, 4) for half in range(HALVES)]]
CHUNKS = [OUTER, MIDDLE, CORE]
PARTS = B // 8

SPEEDS = [
    (0, 0, 0), (1, 0, 0), (-1, 0, 0), (0, 1, 0), (0, -1, 0), (0, 0, 1), (0, 0, -1), (1, 1, 0), (-1, -1, 0), (1, -1, 0),
    (-1, 1, 0), (1, 0, 1), (-1, 0, -1), (1, 0, -1), (-1, 0, 1), (0, 1, 1), (0, -1, -1), (0, 1, -1), (0, -1, 1),
]
ORDER = (
    [d for d in range(Q) if SPEEDS[d][0] == 1]
    + [SOLID]
    + [d for d in range(Q) if SPEEDS[d][0] == 0]
    + [d for d in range(Q) if SPEEDS[d][0] == -1]
)
SLOT = {d: place for place, d in enumerate(ORDER)}
FORWARD = 15

UP_FACE = [
    [(d, 15) for d in range(Q) if SPEEDS[d][2] >= 0] + [(SOLID, 15)],
    [(d, 14) for d in range(Q) if SPEEDS[d][2] == 1],
]
DOWN_FACE = [
    [(d, 0) for d in range(Q) if SPEEDS[d][2] <= 0] + [(SOLID, 0)],
    [(d, 1) for d in range(Q) if SPEEDS[d][2] == -1],
]


def rolled(value, amount):
    amount %= LANES
    return pltpu.roll(value, amount, 1) if amount else value


def collide(f, n):
    pair = {}
    gap = {}
    for i in range(1, Q, 2):
        pair[i] = f[i] + f[i + 1]
        gap[i] = f[i] - f[i + 1]
    xy, xz, yz = pair[7] + pair[9], pair[11] + pair[13], pair[15] + pair[17]
    axes_yz = pair[3] + pair[5]
    axes = pair[1] + axes_yz
    xy_xz = xy + xz
    diagonals = xy_xz + yz
    rho = f[0] + axes + diagonals
    energy = 8.0 * diagonals - 11.0 * axes - 30.0 * f[0]
    energy_2 = diagonals - 4.0 * axes + 12.0 * f[0]
    axial = 2.0 * pair[1] - axes_yz
    planar = xy_xz - 2.0 * yz
    axial_w = pair[3] - pair[5]
    planar_w = xy - xz
    gx_xy, gx_xz = gap[7] + gap[9], gap[11] + gap[13]
    gy_xy, gy_yz = gap[7] - gap[9], gap[15] + gap[17]
    gz_xz, gz_yz = gap[11] - gap[13], gap[15] - gap[17]
    dx, dy, dz = gx_xy + gx_xz, gy_xy + gy_yz, gz_xz + gz_yz
    jx, jy, jz = gap[1] + dx, gap[3] + dy, gap[5] + dz
    third = 1.0 / 3.0
    xx, yy, zz = jx * jx, jy * jy, jz * jz
    yyzz = yy + zz
    square = xx + yyzz
    p = (2.0 * third) * xx - third * yyzz
    w = third * (yy - zz)
    open_share = 1.0 - n

    def relaxed(rate, norm, excess):
        return (rate / norm) * excess

    r_e = open_share * relaxed(1.19, 2394.0, energy + 11.0 * rho - (19.0 * third) * square)
    r_e2 = open_share * relaxed(1.4, 252.0, energy_2 - 3.0 * rho + (5.5 * third) * square)
    r_p = open_share * relaxed(1.25, 36.0, axial + planar - p)
    r_p2 = open_share * relaxed(1.4, 72.0, planar - 2.0 * axial + 0.5 * p)
    r_w = open_share * relaxed(1.25, 12.0, axial_w + planar_w - w)
    r_w2 = open_share * relaxed(1.4, 24.0, planar_w - 2.0 * axial_w + 0.5 * w)
    third_j = (third * jx, third * jy)
    r_xy = open_share * relaxed(1.25, 4.0, pair[7] - pair[9] - third_j[0] * jy)
    r_yz = open_share * relaxed(1.25, 4.0, pair[15] - pair[17] - third_j[1] * jz)
    r_xz = open_share * relaxed(1.25, 4.0, pair[11] - pair[13] - third_j[0] * jz)
    r_qx = open_share * relaxed(1.2, 40.0, dx - 4.0 * gap[1] + (2.0 * third) * jx)
    r_qy = open_share * relaxed(1.2, 40.0, dy - 4.0 * gap[3] + (2.0 * third) * jy)
    r_qz = open_share * relaxed(1.2, 40.0, dz - 4.0 * gap[5] + (2.0 * third) * jz)
    r_mx = open_share * relaxed(1.98, 8.0, gx_xy - gx_xz)
    r_my = open_share * relaxed(1.98, 8.0, gy_yz - gy_xy)
    r_mz = open_share * relaxed(1.98, 8.0, gz_xz - gz_yz)

    even_axis = -11.0 * r_e - 4.0 * r_e2
    even_plane = 8.0 * r_e + r_e2
    a_p = r_p - 2.0 * r_p2
    a_w = r_w - 2.0 * r_w2
    d_p = r_p + r_p2
    d_w = r_w + r_w2
    axis_rest = even_axis - a_p
    plane_x = even_plane + d_p
    even_xy, even_xz, even_yz = plane_x + d_w, plane_x - d_w, even_plane - 2.0 * d_p
    x_plus, x_minus = r_qx + r_mx, r_qx - r_mx
    y_plus, y_minus = r_qy + r_my, r_qy - r_my
    z_plus, z_minus = r_qz + r_mz, r_qz - r_mz
    even = {
        1: even_axis + 2.0 * a_p,
        3: axis_rest + a_w,
        5: axis_rest - a_w,
        7: even_xy + r_xy,
        9: even_xy - r_xy,
        11: even_xz + r_xz,
        13: even_xz - r_xz,
        15: even_yz + r_yz,
        17: even_yz - r_yz,
    }
    odd = {
        1: -4.0 * r_qx,
        3: -4.0 * r_qy,
        5: -4.0 * r_qz,
        7: x_plus + y_minus,
        9: x_plus - y_minus,
        11: x_minus + z_plus,
        13: x_minus - z_plus,
        15: y_plus + z_minus,
        17: y_plus - z_minus,
    }
    post = [f[0] - (12.0 * r_e2 - 30.0 * r_e)]
    for i in range(1, Q, 2):
        turned = n * gap[i] + odd[i]
        post.append(f[i] - even[i] - turned)
        post.append(f[i + 1] - even[i] + turned)
    return post


def gathered(field, slot, block, half, runs, base):
    rows = sum(size for _, size in runs)
    line = lax.broadcasted_iota(jnp.int32, (rows, LANES), 0)
    value, done = None, 0
    for x, size in runs:
        part = field[slot, block, half, pl.ds(base + x - done, rows), :]
        value = part if value is None else jnp.where(line >= done, part, value)
        done += size
    return value


def streamed(field, direction, block, runs, base):
    step_x, step_y, step_z = SPEEDS[direction]
    rows = sum(size for _, size in runs)
    lane = lax.broadcasted_iota(jnp.int32, (rows, LANES), 1)

    def sources(from_block):
        halves = [gathered(field, SLOT[direction], from_block, half, runs, base - step_x) for half in range(HALVES)]
        if step_y == 0:
            return halves
        edge = lane >= LANES - B if step_y == 1 else lane < B
        return [jnp.where(edge, halves[1 - half], halves[half]) for half in range(HALVES)]

    inner = [rolled(value, B * step_y + step_z) for value in sources(block)]
    if step_z == 0:
        return inner
    beside = (block + 3 - step_z) % 3 if isinstance(block, int) else lax.rem(block + 3 - step_z, 3)
    outer = [rolled(value, B * step_y - (B - 1) * step_z) for value in sources(beside)]
    edge = lane % B == (0 if step_z == 1 else B - 1)
    return [jnp.where(edge, *both) for both in zip(outer, inner)]


def packed(face, values):
    lane = lax.broadcasted_iota(jnp.int32, (8, LANES), 1) % B
    out = []
    for items in face:
        total = None
        for slot, (d, z) in enumerate(items):
            value = rolled(values[d], slot - z)
            total = value if total is None else jnp.where(lane == slot, value, total)
        out.append(total)
    return out


def unpacked(up, down):
    lane = lax.broadcasted_iota(jnp.int32, (8, LANES), 1) % B
    out = []
    for d in range(FIELDS):
        total = None
        for face, vregs in ((UP_FACE, up), (DOWN_FACE, down)):
            for items, vreg in zip(face, vregs):
                for slot, (direction, z) in enumerate(items):
                    if direction == d:
                        value = rolled(vreg, z - slot)
                        total = value if total is None else jnp.where(lane == z, value, total)
        out.append(total)
    return out


def kernel(populations, solidity, home_count, evolved, held, counted, *rest):
    chunks = len(CHUNKS)
    sent, arrived = rest[:chunks], rest[chunks : 2 * chunks]
    (
        first, second, up_out, down_out, up_in, down_in,
        load_sem, move_send, move_recv, halo_send, halo_recv,
    ) = rest[2 * chunks :]
    n_grp, n_dev = lax.axis_size("grp"), lax.axis_size("dev")
    grp, dev = lax.axis_index("grp"), lax.axis_index("dev")
    before_g, after_g = lax.rem(grp + n_grp - 1, n_grp), lax.rem(grp + 1, n_grp)
    before_d, after_d = lax.rem(dev + n_dev - 1, n_dev), lax.rem(dev + 1, n_dev)
    before_2, after_2 = lax.rem(dev + n_dev - 2, n_dev), lax.rem(dev + 2, n_dev)
    member = lax.rem(dev, TEAM)
    team = lax.div(dev, TEAM)
    lower_pair = member < TEAM // 2

    loads = [
        pltpu.make_async_copy(home_count, counted, load_sem.at[0]),
        pltpu.make_async_copy(populations, held.at[pl.ds(0, Q * TILES * HS)], load_sem.at[1]),
        pltpu.make_async_copy(solidity, held.at[pl.ds(Q * TILES * HS, TILES * HS)], load_sem.at[2]),
    ]
    for load in loads:
        load.start()
    around = [
        (grp, before_d), (grp, after_d), (before_g, dev), (after_g, dev),
        (grp, jnp.where(lower_pair, after_2, before_2)),
    ]
    barrier = pltpu.get_barrier_semaphore()
    for device in around:
        pl.semaphore_signal(barrier, inc=1, device_id=device, device_id_type=MESH)
    for load in loads:
        load.wait()

    ends = []
    for j in range(TEAM):
        ends.append(counted[0, j, team] + (ends[-1] if ends else 0))
    start = jnp.int32(0)
    for j in range(1, TEAM):
        start = jnp.where(member == j, ends[j - 1], start)

    def holder(block):
        count = jnp.int32(0)
        for j in range(TEAM):
            count = count + (ends[j] <= block).astype(jnp.int32)
        return count

    def home(block):
        return jnp.clip(block - start, 0, HS - 1)

    def from_home(field, half, x, size, slot):
        at = (field * TILES + HALVES * x + half) * HS
        return held[pl.ds(at + slot, size, stride=HS * HALVES), :]

    def stage(target, place, block, index, chunk):
        slot = home(block)
        for field in range(FIELDS):
            to = field * 8 * len(CHUNKS[chunk])
            for vreg in CHUNKS[chunk]:
                for half, x, size in vreg:
                    target[place, index, pl.ds(to, size), :] = from_home(field, half, x, size, slot)
                    to += size

    def to_before(chunk):
        return pltpu.make_async_remote_copy(
            src_ref=sent[chunk].at[0], dst_ref=arrived[chunk].at[2], send_sem=move_send.at[0, chunk],
            recv_sem=move_recv.at[0, chunk], device_id=(grp, before_d), device_id_type=MESH,
        )

    def to_after(chunk):
        return pltpu.make_async_remote_copy(
            src_ref=sent[chunk].at[1], dst_ref=arrived[chunk].at[0], send_sem=move_send.at[1, chunk],
            recv_sem=move_recv.at[1, chunk], device_id=(grp, after_d), device_id_type=MESH,
        )

    def halo(index, source, target, device):
        return pltpu.make_async_remote_copy(
            src_ref=source, dst_ref=target, send_sem=halo_send.at[index], recv_sem=halo_recv.at[index],
            device_id=device, device_id_type=MESH,
        )

    def face_of(face, block, target, place):
        slot = home(block)

        @pl.loop(0, HALVES)
        def _(half):
            for part in range(PARTS):
                f = [from_home(field, half, 8 * part, 8, slot) for field in range(FIELDS)]
                for item, value in enumerate(packed(face, collide(f[:Q], f[SOLID]) + f[Q:])):
                    target[place, item, half, part, :, :] = value

    def up_near():
        return halo(0, up_out.at[0], up_in.at[1], (grp, after_d))

    def up_far():
        return halo(1, up_out.at[1], up_in.at[2], (grp, after_2))

    def down_near():
        return halo(2, down_out.at[0], down_in.at[1], (grp, before_d))

    def down_far():
        return halo(3, down_out.at[1], down_in.at[2], (grp, before_2))

    def move(chunk):
        @pl.when(member > 0)
        def _():
            to_before(chunk).start()

        @pl.when(member < TEAM - 1)
        def _():
            to_after(chunk).start()

    def stage_moves(chunk):
        for index in range(AVG):
            stage(sent[chunk], 0, AVG * (member - 1) + index, index, chunk)
            stage(sent[chunk], 1, AVG * (member + 1) + index, index, chunk)

    stage_moves(0)
    pl.semaphore_wait(barrier, len(around))
    move(0)
    face_of(UP_FACE, AVG * member + 1, up_out, 0)
    up_near().start()
    face_of(DOWN_FACE, AVG * member, down_out, 0)
    down_near().start()

    @pl.when(lower_pair)
    def _():
        face_of(UP_FACE, AVG * member + 3, up_out, 1)
        up_far().start()

    @pl.when(jnp.logical_not(lower_pair))
    def _():
        face_of(DOWN_FACE, AVG * member - 2, down_out, 1)
        down_far().start()

    for chunk in range(1, chunks):
        stage_moves(chunk)
        move(chunk)
    face_of(UP_FACE, AVG * member - 1, up_in, 0)
    face_of(DOWN_FACE, AVG * member + 2, down_in, 0)
    for chunk in range(chunks):
        for index in range(AVG):
            stage(arrived[chunk], 1, AVG * member + index, index, chunk)

    def put(field, block, runs, value):
        done = 0
        for half, x, size in runs:
            first[SLOT[field], block, half, pl.ds(MAIN + x, size), :] = value[done : done + size]
            done += size

    def settle(chunk):
        @pl.when(member > 0)
        def _():
            to_after(chunk).wait_recv()

        @pl.when(member < TEAM - 1)
        def _():
            to_before(chunk).wait_recv()

        box, vregs = arrived[chunk], CHUNKS[chunk]
        for index in range(AVG):
            place = jnp.clip(holder(AVG * member + index) - member + 1, 0, 2)
            for number, runs in enumerate(vregs):
                f = [box[place, index, pl.ds((d * len(vregs) + number) * 8, 8), :] for d in range(FIELDS)]
                post = collide(f[:Q], f[SOLID]) + f[Q:]
                for d, value in enumerate(post):
                    put(d, index, runs, value)

    low, high = pl.ds(MAIN - 2, 2), pl.ds(MAIN + B, 2)
    top, bottom = pl.ds(MAIN + B - 2, 2), pl.ds(MAIN, 2)
    to_g, to_b = pl.ds(0, FORWARD), pl.ds(FIELDS - FORWARD, FORWARD)

    def across(index, blocks):
        return [
            halo(index, first.at[to_g, blocks, :, top, :], first.at[to_g, blocks, :, low, :], (after_g, dev)),
            halo(index + 1, first.at[to_b, blocks, :, bottom, :], first.at[to_b, blocks, :, high, :], (before_g, dev)),
        ]

    def close(lower, upper):
        @pl.loop(0, HALVES)
        def _(half):
            for part in range(PARTS):
                values = unpacked(
                    [up_in[lower, item, half, part, :, :] for item in range(2)],
                    [down_in[upper, item, half, part, :, :] for item in range(2)],
                )
                for d, value in enumerate(values):
                    first[SLOT[d], AVG, half, pl.ds(MAIN + 8 * part, 8), :] = value

    def step(runs):
        def once(block, keep):
            f = [streamed(first, d, block, runs, MAIN) for d in range(Q)]
            for half in range(HALVES):
                n = gathered(first, SLOT[SOLID], block, half, runs, MAIN)
                post = collide([value[half] for value in f], n)
                for d in keep:
                    done = 0
                    for x, size in runs:
                        second[SLOT[d], block, half, pl.ds(x + 1, size), :] = post[d][done : done + size]
                        done += size

        @pl.loop(0, AVG)
        def _(block):
            once(block, range(Q))

        once(AVG, [d for d in range(Q) if SPEEDS[d][2]])

    def finish(runs):
        for block in range(AVG):
            for d in range(Q):
                for half, value in enumerate(streamed(second, d, block, runs, 1)):
                    done = 0
                    for x, size in runs:
                        at = (d * TILES + HALVES * x + half) * AVG + block
                        evolved[pl.ds(at, size, stride=AVG * HALVES), :] = value[done : done + size]
                        done += size

    settle(0)
    outer = across(4, pl.ds(0, AVG))
    for copy in outer:
        copy.start()
    up_near().wait_recv()
    down_near().wait_recv()

    @pl.when(lower_pair)
    def _():
        down_far().wait_recv()

    @pl.when(jnp.logical_not(lower_pair))
    def _():
        up_far().wait_recv()

    lower = jnp.where(member == 0, 1, jnp.clip(member - holder(AVG * member - 1), 0, 2))
    upper = jnp.where(member == TEAM - 1, 1, jnp.clip(holder(AVG * (member + 1)) - member, 0, 2))
    close(lower, upper)
    corners = across(6, pl.ds(AVG, 1))
    for copy in corners:
        copy.start()
    settle(1)
    for copy in outer + corners:
        copy.wait()
    step([(-1, 6), (11, 6)])
    finish([(0, 4), (12, 4)])
    settle(2)
    step([(5, 6)])
    finish([(4, 8)])

    up_near().wait_send()
    down_near().wait_send()

    @pl.when(lower_pair)
    def _():
        up_far().wait_send()

    @pl.when(jnp.logical_not(lower_pair))
    def _():
        down_far().wait_send()

    for chunk in range(chunks):
        @pl.when(member > 0)
        def _():
            to_before(chunk).wait_send()

        @pl.when(member < TEAM - 1)
        def _():
            to_after(chunk).wait_send()


def on_device(populations, solidity, home_count):
    f32 = jnp.float32
    populations = populations.transpose(1, 0, 2).reshape(Q, HS, TILES, LANES).transpose(0, 2, 1, 3).reshape(-1, LANES)
    solidity = solidity.reshape(HS, TILES, LANES).transpose(1, 0, 2).reshape(-1, LANES)
    home_count = home_count.transpose(0, 2, 1)
    arguments = [pltpu.with_memory_space_constraint(a, pltpu.HBM) for a in (populations, solidity, home_count)]

    def boxes(places):
        return [pltpu.VMEM((places, AVG, FIELDS * 8 * len(chunk), LANES), f32) for chunk in CHUNKS]

    def faces(places):
        return [pltpu.VMEM((places, 2, HALVES, PARTS, 8, LANES), f32)] * 2

    evolved = pl.pallas_call(
        kernel,
        out_shape=jax.ShapeDtypeStruct((Q * TILES * AVG, LANES), f32),
        in_specs=[pl.BlockSpec(memory_space=pltpu.HBM)] * 3,
        out_specs=pl.BlockSpec(memory_space=pltpu.VMEM),
        scratch_shapes=[
            pltpu.VMEM((FIELDS * TILES * HS, LANES), f32),
            pltpu.SMEM(home_count.shape, jnp.int32),
            *boxes(2),
            *boxes(3),
            pltpu.VMEM((FIELDS, AVG + 1, HALVES, ROWS, LANES), f32),
            pltpu.VMEM((FIELDS, AVG + 1, HALVES, NEXT_ROWS, LANES), f32),
            *faces(2),
            *faces(3),
            pltpu.SemaphoreType.DMA((3,)),
            pltpu.SemaphoreType.DMA((2, len(CHUNKS))),
            pltpu.SemaphoreType.DMA((2, len(CHUNKS))),
            pltpu.SemaphoreType.DMA((8,)),
            pltpu.SemaphoreType.DMA((8,)),
        ],
        compiler_params=pltpu.CompilerParams(
            collective_id=0, has_side_effects=True, vmem_limit_bytes=48 * 1024 * 1024
        ),
        cost_estimate=pl.CostEstimate(flops=8_000_000, bytes_accessed=3_000_000, transcendentals=0),
    )(*arguments)
    return evolved.reshape(Q, TILES, AVG, LANES).transpose(2, 0, 1, 3).reshape(AVG, Q, C)


def solution(mesh):
    return jax.shard_map(
        on_device,
        mesh=mesh,
        in_specs=(P(("grp", "dev"), None, None), P(("grp", "dev"), None), P("grp", None, None)),
        out_specs=P(("grp", "dev"), None, None),
        check_vma=False,
    )
```

time: 19.1 us -> 17.6 us (0.921)
  the two profiles are of different devices: /device:TPU:1 before, /device:TPU:8 now
where the time goes in v3:
time: 17.6 us; the launch traced here: 17.5 us
  Pallas kernels  16.7 us (95%)
  local copies, waits for them, and re-layouts  0.83 us (5%)
    pallas_call x1, Pallas kernels, on_device(): pl.pallas_call(kernel, out_shape=jax.ShapeDtypeStruct((Q * TILES * AVG, L...  16.7 us
    unnamed x1, local copies, waits for them, and re-layouts  0.83 us

profile of v3, /device:TPU:8, one launch (start us, length us, event | category | flops | bytes accessed | tf_op | source)
XLA Modules:
  0.0 17.5 jit_solution(8966814703241770805)
XLA Ops:
  0.0 16.7 %shard_map.37 = f32[1216,128]{1,0:T(8,128)S(1)} custom-call(f32[2432,128]{1,0:T(8,128)} %bitcast.19, f32[128,128]{1,0:T(8,128)} %bitcast.20, s32[1,4,8]{2,1,0:T(4,128)} %bitcast.21), custom_call_target="tpu_custom_call" | custom-call | flops 8000000 | bytes 3000000 | tf_op jit(solution)/shard_map/pallas_call | solution.py:490
  16.7 0.8 %copy.8 = f32[2,19,4096]{2,0,1:T(2,128)} copy(f32[2,19,4096]{2,0,1:T(2,128)S(1)} %bitcast.18) | data formatting | bytes 1245184

commit v4 on v3

--- a/solution.py
+++ b/solution.py
@@ -212,7 +212,7 @@
     sent, arrived = rest[:chunks], rest[chunks : 2 * chunks]
     (
         first, second, up_out, down_out, up_in, down_in,
-        load_sem, move_send, move_recv, halo_send, halo_recv,
+        load_sem, move_send, move_recv, halo_send, halo_recv, ready,
     ) = rest[2 * chunks :]
     n_grp, n_dev = lax.axis_size("grp"), lax.axis_size("dev")
     grp, dev = lax.axis_index("grp"), lax.axis_index("dev")
@@ -230,13 +230,49 @@
     ]
     for load in loads:
         load.start()
-    around = [
-        (grp, before_d), (grp, after_d), (before_g, dev), (after_g, dev),
-        (grp, jnp.where(lower_pair, after_2, before_2)),
-    ]
     barrier = pltpu.get_barrier_semaphore()
-    for device in around:
-        pl.semaphore_signal(barrier, inc=1, device_id=device, device_id_type=MESH)
+
+    def signal(semaphore, device):
+        pl.semaphore_signal(semaphore, inc=1, device_id=device, device_id_type=MESH)
+
+    signal(barrier, (grp, before_d))
+
+    @pl.when(member < TEAM - 1)
+    def _():
+        signal(barrier, (grp, after_d))
+
+    @pl.when(lower_pair)
+    def _():
+        signal(barrier, (grp, after_2))
+
+    @pl.when(grp < n_grp - 1)
+    def _():
+        signal(barrier, (after_g, dev))
+
+    @pl.when(grp == 0)
+    def _():
+        signal(barrier, (before_g, dev))
+
+    def enter():
+        expected = jnp.minimum(member + 1, 3) + jnp.minimum(grp, 1) + jnp.where(grp == n_grp - 1, 1, 0)
+        pl.semaphore_wait(barrier, expected)
+
+        @pl.when(member == TEAM - 1)
+        def _():
+            signal(ready.at[0], (grp, after_d))
+
+        @pl.when(jnp.logical_not(lower_pair))
+        def _():
+            signal(ready.at[1], (grp, before_2))
+
+        @pl.when(grp > 0)
+        def _():
+            signal(ready.at[2], (before_g, dev))
+
+        @pl.when(grp == n_grp - 1)
+        def _():
+            signal(ready.at[2], (after_g, dev))
+
     for load in loads:
         load.wait()
 
@@ -323,32 +359,60 @@
             stage(sent[chunk], 0, AVG * (member - 1) + index, index, chunk)
             stage(sent[chunk], 1, AVG * (member + 1) + index, index, chunk)
 
+    @pl.when(member == TEAM - 1)
+    def _():
+        face_of(UP_FACE, AVG * member + 1, up_out, 0)
+        enter()
+        up_near().start()
+
     stage_moves(0)
-    pl.semaphore_wait(barrier, len(around))
+
+    @pl.when(member < TEAM - 1)
+    def _():
+        enter()
+
     move(0)
-    face_of(UP_FACE, AVG * member + 1, up_out, 0)
-    up_near().start()
+
+    @pl.when(member < TEAM - 1)
+    def _():
+        face_of(UP_FACE, AVG * member + 1, up_out, 0)
+        up_near().start()
+
     face_of(DOWN_FACE, AVG * member, down_out, 0)
-    down_near().start()
+
+    @pl.when(member > 0)
+    def _():
+        down_near().start()
 
     @pl.when(lower_pair)
     def _():
         face_of(UP_FACE, AVG * member + 3, up_out, 1)
-        up_far().start()
 
     @pl.when(jnp.logical_not(lower_pair))
     def _():
         face_of(DOWN_FACE, AVG * member - 2, down_out, 1)
         down_far().start()
 
-    for chunk in range(1, chunks):
-        stage_moves(chunk)
-        move(chunk)
+    stage_moves(1)
+
+    @pl.when(lower_pair)
+    def _():
+        pl.semaphore_wait(ready.at[1], 1)
+        up_far().start()
+
+    move(1)
+    stage_moves(2)
+    move(2)
     face_of(UP_FACE, AVG * member - 1, up_in, 0)
     face_of(DOWN_FACE, AVG * member + 2, down_in, 0)
     for chunk in range(chunks):
         for index in range(AVG):
             stage(arrived[chunk], 1, AVG * member + index, index, chunk)
+
+    @pl.when(member == 0)
+    def _():
+        pl.semaphore_wait(ready.at[0], 1)
+        down_near().start()
 
     def put(field, block, runs, value):
         done = 0
@@ -424,6 +488,15 @@
                         done += size
 
     settle(0)
+
+    @pl.when(grp == 0)
+    def _():
+        pl.semaphore_wait(ready.at[2], 2)
+
+    @pl.when(jnp.logical_and(grp > 0, grp < n_grp - 1))
+    def _():
+        pl.semaphore_wait(ready.at[2], 1)
+
     outer = across(4, pl.ds(0, AVG))
     for copy in outer:
         copy.start()
@@ -445,13 +518,30 @@
     for copy in corners:
         copy.start()
     settle(1)
-    for copy in outer + corners:
-        copy.wait()
-    step([(-1, 6), (11, 6)])
-    finish([(0, 4), (12, 4)])
-    settle(2)
-    step([(5, 6)])
-    finish([(4, 8)])
+    step([(1, 4), (11, 4)])
+
+    def edges():
+        for copy in outer + corners:
+            copy.wait()
+        step([(-1, 2), (15, 2)])
+        finish([(0, 4), (12, 4)])
+
+    def core():
+        settle(2)
+        step([(5, 6)])
+        finish([(4, 8)])
+
+    inner = jnp.logical_and(member > 0, member < TEAM - 1)
+
+    @pl.when(inner)
+    def _():
+        edges()
+        core()
+
+    @pl.when(jnp.logical_not(inner))
+    def _():
+        core()
+        edges()
 
     up_near().wait_send()
     down_near().wait_send()
@@ -506,6 +596,7 @@
             pltpu.SemaphoreType.DMA((2, len(CHUNKS))),
             pltpu.SemaphoreType.DMA((8,)),
             pltpu.SemaphoreType.DMA((8,)),
+            pltpu.SemaphoreType.REGULAR((3,)),
         ],
         compiler_params=pltpu.CompilerParams(
             collective_id=0, has_side_effects=True, vmem_limit_bytes=48 * 1024 * 1024

time: 17.6 us -> 16.2 us (0.920)
  the two profiles are of different devices: /device:TPU:8 before, /device:TPU:0 now
where the time goes in v4:
time: 16.2 us; the launch traced here: 16 us
  Pallas kernels  15.2 us (94%)
  local copies, waits for them, and re-layouts  0.83 us (5%)
    pallas_call x1, Pallas kernels, on_device(): pl.pallas_call(kernel, out_shape=jax.ShapeDtypeStruct((Q * TILES * AVG, L...  15.2 us
    unnamed x1, local copies, waits for them, and re-layouts  0.83 us

profile of v4, /device:TPU:0, one launch (start us, length us, event | category | flops | bytes accessed | tf_op | source)
XLA Modules:
  0.0 16.0 jit_solution(14630831713119275184)
XLA Ops:
  0.0 15.2 %shard_map.37 = f32[1216,128]{1,0:T(8,128)S(1)} custom-call(f32[2432,128]{1,0:T(8,128)} %bitcast.19, f32[128,128]{1,0:T(8,128)} %bitcast.20, s32[1,4,8]{2,1,0:T(4,128)} %bitcast.21), custom_call_target="tpu_custom_call" | custom-call | flops 8000000 | bytes 3000000 | tf_op jit(solution)/shard_map/pallas_call | solution.py:580
  15.2 0.8 %copy.8 = f32[2,19,4096]{2,0,1:T(2,128)} copy(f32[2,19,4096]{2,0,1:T(2,128)S(1)} %bitcast.18) | data formatting | bytes 1245184

commit v5 on v4

--- a/solution.py
+++ b/solution.py
@@ -40,14 +40,16 @@
 SLOT = {d: place for place, d in enumerate(ORDER)}
 FORWARD = 15
 
-UP_FACE = [
-    [(d, 15) for d in range(Q) if SPEEDS[d][2] >= 0] + [(SOLID, 15)],
-    [(d, 14) for d in range(Q) if SPEEDS[d][2] == 1],
-]
-DOWN_FACE = [
-    [(d, 0) for d in range(Q) if SPEEDS[d][2] <= 0] + [(SOLID, 0)],
-    [(d, 1) for d in range(Q) if SPEEDS[d][2] == -1],
-]
+def face_items(near, far, step):
+    wide = [(d, near) for d in range(Q) if SPEEDS[d][2] != -step] + [(SOLID, near)]
+    thin = [(d, far) for d in range(Q) if SPEEDS[d][2] == step]
+    return [[(half, *item) for item in wide] for half in range(HALVES)] + [
+        [(half, *item) for half in range(HALVES) for item in thin]
+    ]
+
+
+UP_FACE = face_items(B - 1, B - 2, 1)
+DOWN_FACE = face_items(0, 1, -1)
 
 
 def rolled(value, amount):
@@ -185,43 +187,40 @@
     out = []
     for items in face:
         total = None
-        for slot, (d, z) in enumerate(items):
-            value = rolled(values[d], slot - z)
-            total = value if total is None else jnp.where(lane == slot, value, total)
+        for place, (half, d, z) in enumerate(items):
+            value = rolled(values[half][d], place - z)
+            total = value if total is None else jnp.where(lane == place, value, total)
         out.append(total)
     return out
 
 
-def unpacked(up, down):
+def unpacked(faces, half, d):
     lane = lax.broadcasted_iota(jnp.int32, (8, LANES), 1) % B
-    out = []
-    for d in range(FIELDS):
-        total = None
-        for face, vregs in ((UP_FACE, up), (DOWN_FACE, down)):
-            for items, vreg in zip(face, vregs):
-                for slot, (direction, z) in enumerate(items):
-                    if direction == d:
-                        value = rolled(vreg, z - slot)
-                        total = value if total is None else jnp.where(lane == z, value, total)
-        out.append(total)
-    return out
+    total = None
+    for face, vregs in faces:
+        for items, vreg in zip(face, vregs):
+            for place, (of, direction, z) in enumerate(items):
+                if (of, direction) == (half, d):
+                    value = rolled(vreg, z - place)
+                    total = value if total is None else jnp.where(lane == z, value, total)
+    return total
 
 
 def kernel(populations, solidity, home_count, evolved, held, counted, *rest):
     chunks = len(CHUNKS)
     sent, arrived = rest[:chunks], rest[chunks : 2 * chunks]
     (
-        first, second, up_out, down_out, up_in, down_in,
+        first, second, up_out, down_out, relay_out, up_in, down_in, relay_up, relay_down, seam,
         load_sem, move_send, move_recv, halo_send, halo_recv, ready,
     ) = rest[2 * chunks :]
     n_grp, n_dev = lax.axis_size("grp"), lax.axis_size("dev")
     grp, dev = lax.axis_index("grp"), lax.axis_index("dev")
     before_g, after_g = lax.rem(grp + n_grp - 1, n_grp), lax.rem(grp + 1, n_grp)
     before_d, after_d = lax.rem(dev + n_dev - 1, n_dev), lax.rem(dev + 1, n_dev)
-    before_2, after_2 = lax.rem(dev + n_dev - 2, n_dev), lax.rem(dev + 2, n_dev)
     member = lax.rem(dev, TEAM)
     team = lax.div(dev, TEAM)
-    lower_pair = member < TEAM // 2
+    inner = jnp.logical_and(member > 0, member < TEAM - 1)
+    first_dev, last_dev = dev == 0, dev == n_dev - 1
 
     loads = [
         pltpu.make_async_copy(home_count, counted, load_sem.at[0]),
@@ -241,10 +240,6 @@
     def _():
         signal(barrier, (grp, after_d))
 
-    @pl.when(lower_pair)
-    def _():
-        signal(barrier, (grp, after_2))
-
     @pl.when(grp < n_grp - 1)
     def _():
         signal(barrier, (after_g, dev))
@@ -253,25 +248,27 @@
     def _():
         signal(barrier, (before_g, dev))
 
+    @pl.when(first_dev)
+    def _():
+        signal(barrier, (before_g, before_d))
+        signal(barrier, (after_g, before_d))
+
     def enter():
-        expected = jnp.minimum(member + 1, 3) + jnp.minimum(grp, 1) + jnp.where(grp == n_grp - 1, 1, 0)
+        expected = jnp.minimum(member + 1, 2) + jnp.minimum(grp, 1) + jnp.where(grp == n_grp - 1, 1, 0)
+        expected = expected + jnp.where(last_dev, 2, 0)
         pl.semaphore_wait(barrier, expected)
 
         @pl.when(member == TEAM - 1)
         def _():
             signal(ready.at[0], (grp, after_d))
 
-        @pl.when(jnp.logical_not(lower_pair))
-        def _():
-            signal(ready.at[1], (grp, before_2))
-
         @pl.when(grp > 0)
         def _():
-            signal(ready.at[2], (before_g, dev))
+            signal(ready.at[1], (before_g, dev))
 
         @pl.when(grp == n_grp - 1)
         def _():
-            signal(ready.at[2], (after_g, dev))
+            signal(ready.at[1], (after_g, dev))
 
     for load in loads:
         load.wait()
@@ -323,27 +320,40 @@
             device_id=device, device_id_type=MESH,
         )
 
-    def face_of(face, block, target, place):
+    def face_of(face, block, target):
         slot = home(block)
 
-        @pl.loop(0, HALVES)
-        def _(half):
+        @pl.loop(0, PARTS)
+        def _(part):
+            values = []
+            for half in range(HALVES):
+                f = [from_home(field, half, 8 * part, 8, slot) for field in range(FIELDS)]
+                values.append(collide(f[:Q], f[SOLID]) + f[Q:])
+            for item, value in enumerate(packed(face, values)):
+                target[item, part, :, :] = value
+
+    def up_face():
+        return halo(0, up_out, up_in.at[1], (grp, after_d))
+
+    def down_face():
+        return halo(1, down_out, down_in.at[1], (grp, before_d))
+
+    def pass_up():
+        return halo(2, relay_out, relay_up, (grp, after_d))
+
+    def pass_down():
+        return halo(3, relay_out, relay_down, (grp, before_d))
+
+    def passed(target, box, cond):
+        for item in range(len(UP_FACE)):
             for part in range(PARTS):
-                f = [from_home(field, half, 8 * part, 8, slot) for field in range(FIELDS)]
-                for item, value in enumerate(packed(face, collide(f[:Q], f[SOLID]) + f[Q:])):
-                    target[place, item, half, part, :, :] = value
-
-    def up_near():
-        return halo(0, up_out.at[0], up_in.at[1], (grp, after_d))
-
-    def up_far():
-        return halo(1, up_out.at[1], up_in.at[2], (grp, after_2))
-
-    def down_near():
-        return halo(2, down_out.at[0], down_in.at[1], (grp, before_d))
-
-    def down_far():
-        return halo(3, down_out.at[1], down_in.at[2], (grp, before_2))
+                target[item, part, :, :] = jnp.where(cond, box[item, part, :, :], target[item, part, :, :])
+
+    def seam_copies():
+        return [
+            halo(8, up_out.at[:, PARTS - 1, pl.ds(6, 2), :], seam.at[:, pl.ds(0, 2), :], (after_g, after_d)),
+            halo(9, up_out.at[:, 0, pl.ds(0, 2), :], seam.at[:, pl.ds(2, 2), :], (before_g, after_d)),
+        ]
 
     def move(chunk):
         @pl.when(member > 0)
@@ -359,60 +369,83 @@
             stage(sent[chunk], 0, AVG * (member - 1) + index, index, chunk)
             stage(sent[chunk], 1, AVG * (member + 1) + index, index, chunk)
 
+    low, high = AVG * member, AVG * member + AVG - 1
+
     @pl.when(member == TEAM - 1)
     def _():
-        face_of(UP_FACE, AVG * member + 1, up_out, 0)
+        face_of(UP_FACE, high, up_out)
         enter()
-        up_near().start()
+        up_face().start()
+
+        @pl.when(last_dev)
+        def _():
+            for copy in seam_copies():
+                copy.start()
+
+        face_of(DOWN_FACE, low - AVG, relay_out)
+        pass_down().start()
+        face_of(DOWN_FACE, low, down_out)
+        down_face().start()
+
+    @pl.when(member == 0)
+    def _():
+        face_of(UP_FACE, high + AVG, relay_out)
+        enter()
+        pass_up().start()
+        face_of(UP_FACE, high, up_out)
+        up_face().start()
 
     stage_moves(0)
 
-    @pl.when(member < TEAM - 1)
+    @pl.when(inner)
     def _():
         enter()
 
     move(0)
 
-    @pl.when(member < TEAM - 1)
-    def _():
-        face_of(UP_FACE, AVG * member + 1, up_out, 0)
-        up_near().start()
-
-    face_of(DOWN_FACE, AVG * member, down_out, 0)
-
-    @pl.when(member > 0)
-    def _():
-        down_near().start()
-
-    @pl.when(lower_pair)
-    def _():
-        face_of(UP_FACE, AVG * member + 3, up_out, 1)
-
-    @pl.when(jnp.logical_not(lower_pair))
-    def _():
-        face_of(DOWN_FACE, AVG * member - 2, down_out, 1)
-        down_far().start()
+    @pl.when(member == 1)
+    def _():
+        face_of(UP_FACE, high + AVG, relay_out)
+        pass_up().start()
+        face_of(UP_FACE, high, up_out)
+
+    @pl.when(member == 2)
+    def _():
+        face_of(DOWN_FACE, low - AVG, relay_out)
+        pass_down().start()
+        face_of(DOWN_FACE, low, down_out)
 
     stage_moves(1)
 
-    @pl.when(lower_pair)
-    def _():
-        pl.semaphore_wait(ready.at[1], 1)
-        up_far().start()
+    @pl.when(member == 1)
+    def _():
+        pass_up().wait_recv()
+        passed(up_out, relay_up, holder(high) < member)
+        up_face().start()
+
+    @pl.when(member == 2)
+    def _():
+        pass_down().wait_recv()
+        passed(down_out, relay_down, holder(low) > member)
+        down_face().start()
 
     move(1)
     stage_moves(2)
     move(2)
-    face_of(UP_FACE, AVG * member - 1, up_in, 0)
-    face_of(DOWN_FACE, AVG * member + 2, down_in, 0)
+
+    @pl.when(member < 2)
+    def _():
+        face_of(DOWN_FACE, low, down_out)
+
+    @pl.when(member == 2)
+    def _():
+        face_of(UP_FACE, high, up_out)
+
+    face_of(UP_FACE, low - 1, up_in.at[0])
+    face_of(DOWN_FACE, high + 1, down_in.at[0])
     for chunk in range(chunks):
         for index in range(AVG):
-            stage(arrived[chunk], 1, AVG * member + index, index, chunk)
-
-    @pl.when(member == 0)
-    def _():
-        pl.semaphore_wait(ready.at[0], 1)
-        down_near().start()
+            stage(arrived[chunk], 1, low + index, index, chunk)
 
     def put(field, block, runs, value):
         done = 0
@@ -438,26 +471,47 @@
                 for d, value in enumerate(post):
                     put(d, index, runs, value)
 
-    low, high = pl.ds(MAIN - 2, 2), pl.ds(MAIN + B, 2)
+    below, above = pl.ds(MAIN - 2, 2), pl.ds(MAIN + B, 2)
     top, bottom = pl.ds(MAIN + B - 2, 2), pl.ds(MAIN, 2)
     to_g, to_b = pl.ds(0, FORWARD), pl.ds(FIELDS - FORWARD, FORWARD)
 
     def across(index, blocks):
         return [
-            halo(index, first.at[to_g, blocks, :, top, :], first.at[to_g, blocks, :, low, :], (after_g, dev)),
-            halo(index + 1, first.at[to_b, blocks, :, bottom, :], first.at[to_b, blocks, :, high, :], (before_g, dev)),
+            halo(index, first.at[to_g, blocks, :, top, :], first.at[to_g, blocks, :, below, :], (after_g, dev)),
+            halo(index + 1, first.at[to_b, blocks, :, bottom, :], first.at[to_b, blocks, :, above, :], (before_g, dev)),
         ]
 
-    def close(lower, upper):
-        @pl.loop(0, HALVES)
-        def _(half):
-            for part in range(PARTS):
-                values = unpacked(
-                    [up_in[lower, item, half, part, :, :] for item in range(2)],
-                    [down_in[upper, item, half, part, :, :] for item in range(2)],
-                )
-                for d, value in enumerate(values):
-                    first[SLOT[d], AVG, half, pl.ds(MAIN + 8 * part, 8), :] = value
+    def close(up, down):
+        kept = lax.broadcasted_iota(jnp.int32, (8, LANES), 1) % B < B // 2
+        for part in range(PARTS):
+            rows = pl.ds(MAIN + 8 * part, 8)
+            faces = []
+            if up is not None:
+                faces.append((UP_FACE, [up_in[up, item, part, :, :] for item in range(len(UP_FACE))]))
+            if down is not None:
+                faces.append((DOWN_FACE, [down_in[down, item, part, :, :] for item in range(len(DOWN_FACE))]))
+            for half in range(HALVES):
+                for d in range(FIELDS):
+                    value = unpacked(faces, half, d)
+                    if value is None:
+                        continue
+                    if down is None and not (d < Q and SPEEDS[d][2] == 1):
+                        value = jnp.where(kept, first[SLOT[d], AVG, half, rows, :], value)
+                    first[SLOT[d], AVG, half, rows, :] = value
+
+    def close_seam():
+        vregs = [seam[item, :, :] for item in range(len(UP_FACE))]
+        kept = lax.broadcasted_iota(jnp.int32, (2, LANES), 1) % B < B // 2
+        for half in range(HALVES):
+            for d in range(FIELDS):
+                value = unpacked([(UP_FACE, vregs)], half, d)
+                if value is None:
+                    continue
+                for done, rows in ((0, below), (2, above)):
+                    part = value[done : done + 2]
+                    if not (d < Q and SPEEDS[d][2] == 1):
+                        part = jnp.where(kept, first[SLOT[d], AVG, half, rows, :], part)
+                    first[SLOT[d], AVG, half, rows, :] = part
 
     def step(runs):
         def once(block, keep):
@@ -471,10 +525,8 @@
                         second[SLOT[d], block, half, pl.ds(x + 1, size), :] = post[d][done : done + size]
                         done += size
 
-        @pl.loop(0, AVG)
-        def _(block):
+        for block in range(AVG):
             once(block, range(Q))
-
         once(AVG, [d for d in range(Q) if SPEEDS[d][2]])
 
     def finish(runs):
@@ -491,38 +543,74 @@
 
     @pl.when(grp == 0)
     def _():
-        pl.semaphore_wait(ready.at[2], 2)
+        pl.semaphore_wait(ready.at[1], 2)
 
     @pl.when(jnp.logical_and(grp > 0, grp < n_grp - 1))
     def _():
-        pl.semaphore_wait(ready.at[2], 1)
+        pl.semaphore_wait(ready.at[1], 1)
 
     outer = across(4, pl.ds(0, AVG))
     for copy in outer:
         copy.start()
-    up_near().wait_recv()
-    down_near().wait_recv()
-
-    @pl.when(lower_pair)
-    def _():
-        down_far().wait_recv()
-
-    @pl.when(jnp.logical_not(lower_pair))
-    def _():
-        up_far().wait_recv()
-
-    lower = jnp.where(member == 0, 1, jnp.clip(member - holder(AVG * member - 1), 0, 2))
-    upper = jnp.where(member == TEAM - 1, 1, jnp.clip(holder(AVG * (member + 1)) - member, 0, 2))
-    close(lower, upper)
+    @pl.when(member == 0)
+    def _():
+        pl.semaphore_wait(ready.at[0], 1)
+        down_face().start()
+
+    @pl.when(member == 1)
+    def _():
+        pass_down().wait_recv()
+        passed(down_out, relay_down, holder(low) > member)
+        down_face().start()
+
+    @pl.when(member == 2)
+    def _():
+        pass_up().wait_recv()
+        passed(up_out, relay_up, holder(high) < member)
+        up_face().start()
+
+    lower = jnp.where(jnp.logical_and(member > 0, holder(low - 1) == member), 0, 1)
+    upper = jnp.where(jnp.logical_and(member < TEAM - 1, holder(high + 1) == member), 0, 1)
     corners = across(6, pl.ds(AVG, 1))
-    for copy in corners:
-        copy.start()
+    down_face().wait_recv()
+
+    @pl.when(first_dev)
+    def _():
+        close(None, upper)
+        for copy in corners:
+            copy.start()
+        for copy in corners:
+            copy.wait_send()
+        up_face().wait_recv()
+        close(lower, None)
+
+    @pl.when(jnp.logical_not(first_dev))
+    def _():
+        up_face().wait_recv()
+        close(lower, upper)
+        for copy in corners:
+            copy.start()
+
     settle(1)
     step([(1, 4), (11, 4)])
 
     def edges():
-        for copy in outer + corners:
+        for copy in outer:
             copy.wait()
+        for copy in corners:
+            copy.wait_recv()
+
+        @pl.when(first_dev)
+        def _():
+            for copy in seam_copies():
+                copy.wait_recv()
+            close_seam()
+
+        @pl.when(jnp.logical_not(first_dev))
+        def _():
+            for copy in corners:
+                copy.wait_send()
+
         step([(-1, 2), (15, 2)])
         finish([(0, 4), (12, 4)])
 
@@ -531,8 +619,6 @@
         step([(5, 6)])
         finish([(4, 8)])
 
-    inner = jnp.logical_and(member > 0, member < TEAM - 1)
-
     @pl.when(inner)
     def _():
         edges()
@@ -543,16 +629,21 @@
         core()
         edges()
 
-    up_near().wait_send()
-    down_near().wait_send()
-
-    @pl.when(lower_pair)
-    def _():
-        up_far().wait_send()
-
-    @pl.when(jnp.logical_not(lower_pair))
-    def _():
-        down_far().wait_send()
+    up_face().wait_send()
+    down_face().wait_send()
+
+    @pl.when(member < 2)
+    def _():
+        pass_up().wait_send()
+
+    @pl.when(member >= 2)
+    def _():
+        pass_down().wait_send()
+
+    @pl.when(last_dev)
+    def _():
+        for copy in seam_copies():
+            copy.wait_send()
 
     for chunk in range(chunks):
         @pl.when(member > 0)
@@ -574,8 +665,8 @@
     def boxes(places):
         return [pltpu.VMEM((places, AVG, FIELDS * 8 * len(chunk), LANES), f32) for chunk in CHUNKS]
 
-    def faces(places):
-        return [pltpu.VMEM((places, 2, HALVES, PARTS, 8, LANES), f32)] * 2
+    def faces(*places):
+        return pltpu.VMEM((*places, len(UP_FACE), PARTS, 8, LANES), f32)
 
     evolved = pl.pallas_call(
         kernel,
@@ -589,14 +680,16 @@
             *boxes(3),
             pltpu.VMEM((FIELDS, AVG + 1, HALVES, ROWS, LANES), f32),
             pltpu.VMEM((FIELDS, AVG + 1, HALVES, NEXT_ROWS, LANES), f32),
-            *faces(2),
-            *faces(3),
+            *[faces() for _ in range(3)],
+            *[faces(2) for _ in range(2)],
+            *[faces() for _ in range(2)],
+            pltpu.VMEM((len(UP_FACE), 8, LANES), f32),
             pltpu.SemaphoreType.DMA((3,)),
             pltpu.SemaphoreType.DMA((2, len(CHUNKS))),
             pltpu.SemaphoreType.DMA((2, len(CHUNKS))),
-            pltpu.SemaphoreType.DMA((8,)),
-            pltpu.SemaphoreType.DMA((8,)),
-            pltpu.SemaphoreType.REGULAR((3,)),
+            pltpu.SemaphoreType.DMA((10,)),
+            pltpu.SemaphoreType.DMA((10,)),
+            pltpu.SemaphoreType.REGULAR((2,)),
         ],
         compiler_params=pltpu.CompilerParams(
             collective_id=0, has_side_effects=True, vmem_limit_bytes=48 * 1024 * 1024

time: 16.2 us -> 15.1 us (0.932)
  the two profiles are of different devices: /device:TPU:0 before, /device:TPU:1 now
where the time goes in v5:
time: 15.1 us; the launch traced here: 15 us
  Pallas kernels  14.2 us (94%)
  local copies, waits for them, and re-layouts  0.83 us (5%)
    pallas_call x1, Pallas kernels, on_device(): pl.pallas_call(kernel, out_shape=jax.ShapeDtypeStruct((Q * TILES * AVG, L...  14.2 us
    unnamed x1, local copies, waits for them, and re-layouts  0.83 us

profile of v5, /device:TPU:1, one launch (start us, length us, event | category | flops | bytes accessed | tf_op | source)
XLA Modules:
  0.0 15.0 jit_solution(325132929394846014)
XLA Ops:
  0.0 14.2 %shard_map.37 = f32[1216,128]{1,0:T(8,128)S(1)} custom-call(f32[2432,128]{1,0:T(8,128)} %bitcast.19, f32[128,128]{1,0:T(8,128)} %bitcast.20, s32[1,4,8]{2,1,0:T(4,128)} %bitcast.21), custom_call_target="tpu_custom_call" | custom-call | flops 8000000 | bytes 3000000 | tf_op jit(solution)/shard_map/pallas_call | solution.py:671
  14.2 0.8 %copy.8 = f32[2,19,4096]{2,0,1:T(2,128)} copy(f32[2,19,4096]{2,0,1:T(2,128)S(1)} %bitcast.18) | data formatting | bytes 1245184

commit v6 on v5

--- a/solution.py
+++ b/solution.py
@@ -21,11 +21,25 @@
 MAIN = 8
 ROWS = 32
 NEXT_ROWS = 24
-OUTER = [[(half, x, 2) for half in range(HALVES) for x in (0, 14)]]
-MIDDLE = [[(half, 2, 4), (half, 10, 4)] for half in range(HALVES)]
-CORE = [[(half, 6, 4) for half in range(HALVES)]]
-CHUNKS = [OUTER, MIDDLE, CORE]
+def pairs(first, last, size):
+    return [(half, x, size) for x in (first, last) for half in range(HALVES)]
+
+
+def halves(*runs):
+    return [[(half, *run) for run in runs] for half in range(HALVES)]
+
+
+CHUNKS = [[pairs(0, 14, 2)], halves((2, 3), (11, 3)), [pairs(5, 9, 2)], [[(half, 7, 2) for half in range(HALVES)]]]
 PARTS = B // 8
+FIELD_ROWS = TILES * HS
+EDGE = 2 * HALVES * HS
+
+
+def length(runs):
+    return sum(size for _, _, size in runs)
+
+
+DEPTH = [sum(length(runs) for runs in chunk) for chunk in CHUNKS]
 
 SPEEDS = [
     (0, 0, 0), (1, 0, 0), (-1, 0, 0), (0, 1, 0), (0, -1, 0), (0, 0, 1), (0, 0, -1), (1, 1, 0), (-1, -1, 0), (1, -1, 0),
@@ -150,36 +164,40 @@
     return post
 
 
-def gathered(field, slot, block, half, runs, base):
-    rows = sum(size for _, size in runs)
+def gathered(field, slot, block, runs, base):
+    rows = length(runs)
     line = lax.broadcasted_iota(jnp.int32, (rows, LANES), 0)
     value, done = None, 0
-    for x, size in runs:
+    for half, x, size in runs:
+        assert 0 <= base + x - done <= field.shape[3] - rows
         part = field[slot, block, half, pl.ds(base + x - done, rows), :]
         value = part if value is None else jnp.where(line >= done, part, value)
         done += size
     return value
 
 
-def streamed(field, direction, block, runs, base):
+def streamed(field, direction, block, runs, base, known):
     step_x, step_y, step_z = SPEEDS[direction]
-    rows = sum(size for _, size in runs)
-    lane = lax.broadcasted_iota(jnp.int32, (rows, LANES), 1)
-
-    def sources(from_block):
-        halves = [gathered(field, SLOT[direction], from_block, half, runs, base - step_x) for half in range(HALVES)]
+    lane = lax.broadcasted_iota(jnp.int32, (length(runs), LANES), 1)
+
+    def rows_of(from_block, from_runs):
+        key = (direction, from_block, tuple(from_runs))
+        if key not in known:
+            known[key] = gathered(field, SLOT[direction], from_block, from_runs, base - step_x)
+        return known[key]
+
+    def source(from_block):
+        own = rows_of(from_block, runs)
         if step_y == 0:
-            return halves
+            return own
         edge = lane >= LANES - B if step_y == 1 else lane < B
-        return [jnp.where(edge, halves[1 - half], halves[half]) for half in range(HALVES)]
-
-    inner = [rolled(value, B * step_y + step_z) for value in sources(block)]
+        return jnp.where(edge, rows_of(from_block, [(1 - half, x, size) for half, x, size in runs]), own)
+
+    inner = rolled(source(block), B * step_y + step_z)
     if step_z == 0:
         return inner
-    beside = (block + 3 - step_z) % 3 if isinstance(block, int) else lax.rem(block + 3 - step_z, 3)
-    outer = [rolled(value, B * step_y - (B - 1) * step_z) for value in sources(beside)]
-    edge = lane % B == (0 if step_z == 1 else B - 1)
-    return [jnp.where(edge, *both) for both in zip(outer, inner)]
+    outer = rolled(source((block + 3 - step_z) % 3), B * step_y - (B - 1) * step_z)
+    return jnp.where(lane % B == (0 if step_z == 1 else B - 1), outer, inner)
 
 
 def packed(face, values):
@@ -206,7 +224,7 @@
     return total
 
 
-def kernel(populations, solidity, home_count, evolved, held, counted, *rest):
+def kernel(populations, solidity, home_count, evolved, held, outermost, counted, *rest):
     chunks = len(CHUNKS)
     sent, arrived = rest[:chunks], rest[chunks : 2 * chunks]
     (
@@ -222,11 +240,14 @@
     inner = jnp.logical_and(member > 0, member < TEAM - 1)
     first_dev, last_dev = dev == 0, dev == n_dev - 1
 
-    loads = [
-        pltpu.make_async_copy(home_count, counted, load_sem.at[0]),
-        pltpu.make_async_copy(populations, held.at[pl.ds(0, Q * TILES * HS)], load_sem.at[1]),
-        pltpu.make_async_copy(solidity, held.at[pl.ds(Q * TILES * HS, TILES * HS)], load_sem.at[2]),
-    ]
+    edge_rows = [(pl.ds(0, EDGE), pl.ds(0, EDGE)), (pl.ds(FIELD_ROWS - EDGE, EDGE), pl.ds(EDGE, EDGE))]
+    whole = pl.ds(0, FIELD_ROWS)
+    loads = [pltpu.make_async_copy(home_count, counted, load_sem.at[0])]
+    for number, (rows, place, to) in enumerate([(*edge_rows[0], outermost), (*edge_rows[1], outermost), (whole, whole, held)]):
+        loads.append(
+            pltpu.make_async_copy(populations.at[:, rows], to.at[pl.ds(0, Q), place], load_sem.at[2 * number + 1])
+        )
+        loads.append(pltpu.make_async_copy(solidity.at[rows], to.at[SOLID, place], load_sem.at[2 * number + 2]))
     for load in loads:
         load.start()
     barrier = pltpu.get_barrier_semaphore()
@@ -270,7 +291,7 @@
         def _():
             signal(ready.at[1], (after_g, dev))
 
-    for load in loads:
+    for load in loads[:-2]:
         load.wait()
 
     ends = []
@@ -290,16 +311,20 @@
         return jnp.clip(block - start, 0, HS - 1)
 
     def from_home(field, half, x, size, slot):
-        at = (field * TILES + HALVES * x + half) * HS
-        return held[pl.ds(at + slot, size, stride=HS * HALVES), :]
+        return held[field, pl.ds((HALVES * x + half) * HS + slot, size, stride=HS * HALVES), :]
 
     def stage(target, place, block, index, chunk):
         slot = home(block)
         for field in range(FIELDS):
-            to = field * 8 * len(CHUNKS[chunk])
+            to = field * DEPTH[chunk]
             for vreg in CHUNKS[chunk]:
                 for half, x, size in vreg:
-                    target[place, index, pl.ds(to, size), :] = from_home(field, half, x, size, slot)
+                    if chunk == 0:
+                        at = (HALVES * (x if x < 2 else x - B + 4) + half) * HS
+                        value = outermost[field, pl.ds(at + slot, size, stride=HS * HALVES), :]
+                    else:
+                        value = from_home(field, half, x, size, slot)
+                    target[place, index, pl.ds(to, size), :] = value
                     to += size
 
     def to_before(chunk):
@@ -371,6 +396,14 @@
 
     low, high = AVG * member, AVG * member + AVG - 1
 
+    def rest_loaded():
+        for load in loads[-2:]:
+            load.wait()
+
+    @pl.when(jnp.logical_not(inner))
+    def _():
+        rest_loaded()
+
     @pl.when(member == TEAM - 1)
     def _():
         face_of(UP_FACE, high, up_out)
@@ -403,6 +436,10 @@
 
     move(0)
 
+    @pl.when(inner)
+    def _():
+        rest_loaded()
+
     @pl.when(member == 1)
     def _():
         face_of(UP_FACE, high + AVG, relay_out)
@@ -430,8 +467,9 @@
         down_face().start()
 
     move(1)
-    stage_moves(2)
-    move(2)
+    for chunk in range(2, chunks):
+        stage_moves(chunk)
+        move(chunk)
 
     @pl.when(member < 2)
     def _():
@@ -462,14 +500,15 @@
         def _():
             to_before(chunk).wait_recv()
 
-        box, vregs = arrived[chunk], CHUNKS[chunk]
+        box = arrived[chunk]
         for index in range(AVG):
             place = jnp.clip(holder(AVG * member + index) - member + 1, 0, 2)
-            for number, runs in enumerate(vregs):
-                f = [box[place, index, pl.ds((d * len(vregs) + number) * 8, 8), :] for d in range(FIELDS)]
-                post = collide(f[:Q], f[SOLID]) + f[Q:]
-                for d, value in enumerate(post):
+            done = 0
+            for runs in CHUNKS[chunk]:
+                f = [box[place, index, pl.ds(d * DEPTH[chunk] + done, length(runs)), :] for d in range(FIELDS)]
+                for d, value in enumerate(collide(f[:Q], f[SOLID]) + f[Q:]):
                     put(d, index, runs, value)
+                done += length(runs)
 
     below, above = pl.ds(MAIN - 2, 2), pl.ds(MAIN + B, 2)
     top, bottom = pl.ds(MAIN + B - 2, 2), pl.ds(MAIN, 2)
@@ -513,28 +552,26 @@
                         part = jnp.where(kept, first[SLOT[d], AVG, half, rows, :], part)
                     first[SLOT[d], AVG, half, rows, :] = part
 
-    def step(runs):
-        def once(block, keep):
-            f = [streamed(first, d, block, runs, MAIN) for d in range(Q)]
-            for half in range(HALVES):
-                n = gathered(first, SLOT[SOLID], block, half, runs, MAIN)
-                post = collide([value[half] for value in f], n)
-                for d in keep:
+    def step(groups):
+        for block in range(AVG + 1):
+            known = {}
+            arriving = [[streamed(first, d, block, runs, MAIN, known) for d in range(Q)] for runs in groups]
+            for runs, f in zip(groups, arriving):
+                post = collide(f, gathered(first, SLOT[SOLID], block, runs, MAIN))
+                for d in range(Q):
                     done = 0
-                    for x, size in runs:
-                        second[SLOT[d], block, half, pl.ds(x + 1, size), :] = post[d][done : done + size]
+                    for half, x, size in runs:
+                        if block < AVG or SPEEDS[d][2]:
+                            second[SLOT[d], block, half, pl.ds(x + 1, size), :] = post[d][done : done + size]
                         done += size
 
+    def finish(groups):
         for block in range(AVG):
-            once(block, range(Q))
-        once(AVG, [d for d in range(Q) if SPEEDS[d][2]])
-
-    def finish(runs):
-        for block in range(AVG):
+            known = {}
             for d in range(Q):
-                for half, value in enumerate(streamed(second, d, block, runs, 1)):
-                    done = 0
-                    for x, size in runs:
+                for runs in groups:
+                    value, done = streamed(second, d, block, runs, 1, known), 0
+                    for half, x, size in runs:
                         at = (d * TILES + HALVES * x + half) * AVG + block
                         evolved[pl.ds(at, size, stride=AVG * HALVES), :] = value[done : done + size]
                         done += size
@@ -592,7 +629,7 @@
             copy.start()
 
     settle(1)
-    step([(1, 4), (11, 4)])
+    step(halves((1, 3), (12, 3)))
 
     def edges():
         for copy in outer:
@@ -611,13 +648,16 @@
             for copy in corners:
                 copy.wait_send()
 
-        step([(-1, 2), (15, 2)])
-        finish([(0, 4), (12, 4)])
+        step([pairs(-1, 15, 2)])
+        finish(halves((0, 3), (13, 3)))
 
     def core():
         settle(2)
-        step([(5, 6)])
-        finish([(4, 8)])
+        step([pairs(4, 10, 2)])
+        finish([pairs(3, 11, 2)])
+        settle(3)
+        step([[(half, 6, 4) for half in range(HALVES)]])
+        finish(halves((5, 6)))
 
     @pl.when(inner)
     def _():
@@ -657,13 +697,14 @@
 
 def on_device(populations, solidity, home_count):
     f32 = jnp.float32
-    populations = populations.transpose(1, 0, 2).reshape(Q, HS, TILES, LANES).transpose(0, 2, 1, 3).reshape(-1, LANES)
+    populations = populations.transpose(1, 0, 2).reshape(Q, HS, TILES, LANES).transpose(0, 2, 1, 3)
+    populations = populations.reshape(Q, FIELD_ROWS, LANES)
     solidity = solidity.reshape(HS, TILES, LANES).transpose(1, 0, 2).reshape(-1, LANES)
     home_count = home_count.transpose(0, 2, 1)
     arguments = [pltpu.with_memory_space_constraint(a, pltpu.HBM) for a in (populations, solidity, home_count)]
 
     def boxes(places):
-        return [pltpu.VMEM((places, AVG, FIELDS * 8 * len(chunk), LANES), f32) for chunk in CHUNKS]
+        return [pltpu.VMEM((places, AVG, FIELDS * depth, LANES), f32) for depth in DEPTH]
 
     def faces(*places):
         return pltpu.VMEM((*places, len(UP_FACE), PARTS, 8, LANES), f32)
@@ -674,7 +715,8 @@
         in_specs=[pl.BlockSpec(memory_space=pltpu.HBM)] * 3,
         out_specs=pl.BlockSpec(memory_space=pltpu.VMEM),
         scratch_shapes=[
-            pltpu.VMEM((FIELDS * TILES * HS, LANES), f32),
+            pltpu.VMEM((FIELDS, FIELD_ROWS, LANES), f32),
+            pltpu.VMEM((FIELDS, 2 * EDGE, LANES), f32),
             pltpu.SMEM(home_count.shape, jnp.int32),
             *boxes(2),
             *boxes(3),
@@ -684,7 +726,7 @@
             *[faces(2) for _ in range(2)],
             *[faces() for _ in range(2)],
             pltpu.VMEM((len(UP_FACE), 8, LANES), f32),
-            pltpu.SemaphoreType.DMA((3,)),
+            pltpu.SemaphoreType.DMA((7,)),
             pltpu.SemaphoreType.DMA((2, len(CHUNKS))),
             pltpu.SemaphoreType.DMA((2, len(CHUNKS))),
             pltpu.SemaphoreType.DMA((10,)),

time: 15.1 us -> 14.7 us (0.974)
  Pallas kernels: 14.2 us -> 13.8 us
    pallas_call x1, Pallas kernels: 14.2 us -> 13.8 us  [on_device(): pl.pallas_call(kernel, out_shape=jax.ShapeDtypeStruct((Q * TILES * AVG, L...]
where the time goes in v6:
time: 14.7 us; the launch traced here: 14.6 us
  Pallas kernels  13.8 us (94%)
  local copies, waits for them, and re-layouts  0.83 us (6%)
    pallas_call x1, Pallas kernels, on_device(): pl.pallas_call(kernel, out_shape=jax.ShapeDtypeStruct((Q * TILES * AVG, L...  13.8 us
    unnamed x1, local copies, waits for them, and re-layouts  0.83 us

profile of v6, /device:TPU:1, one launch (start us, length us, event | category | flops | bytes accessed | tf_op | source)
XLA Modules:
  0.0 14.6 jit_solution(991661858644302379)
XLA Ops:
  0.0 13.8 %shard_map.37 = f32[1216,128]{1,0:T(8,128)S(1)} custom-call(f32[19,128,128]{2,1,0:T(8,128)} %bitcast.19, f32[128,128]{1,0:T(8,128)} %bitcast.20, s32[1,4,8]{2,1,0:T(4,128)} %bitcast.21), custom_call_target="tpu_custom_call" | custom-call | flops 8000000 | bytes 3000000 | tf_op jit(solution)/shard_map/pallas_call | solution.py:712
  13.8 0.8 %copy.8 = f32[2,19,4096]{2,0,1:T(2,128)} copy(f32[2,19,4096]{2,0,1:T(2,128)S(1)} %bitcast.18) | data formatting | bytes 1245184

commit v7 on v6

--- a/solution.py
+++ b/solution.py
@@ -20,7 +20,6 @@
 HALVES = 2
 MAIN = 8
 ROWS = 32
-NEXT_ROWS = 24
 def pairs(first, last, size):
     return [(half, x, size) for x in (first, last) for half in range(HALVES)]
 
@@ -279,6 +278,7 @@
         expected = expected + jnp.where(last_dev, 2, 0)
         pl.semaphore_wait(barrier, expected)
 
+    def answer():
         @pl.when(member == TEAM - 1)
         def _():
             signal(ready.at[0], (grp, after_d))
@@ -389,10 +389,13 @@
         def _():
             to_after(chunk).start()
 
+    def stage_move(chunk, place):
+        for index in range(AVG):
+            stage(sent[chunk], place, AVG * (member - 1 + 2 * place) + index, index, chunk)
+
     def stage_moves(chunk):
-        for index in range(AVG):
-            stage(sent[chunk], 0, AVG * (member - 1) + index, index, chunk)
-            stage(sent[chunk], 1, AVG * (member + 1) + index, index, chunk)
+        stage_move(chunk, 0)
+        stage_move(chunk, 1)
 
     low, high = AVG * member, AVG * member + AVG - 1
 
@@ -415,6 +418,7 @@
             for copy in seam_copies():
                 copy.start()
 
+        answer()
         face_of(DOWN_FACE, low - AVG, relay_out)
         pass_down().start()
         face_of(DOWN_FACE, low, down_out)
@@ -425,19 +429,34 @@
         face_of(UP_FACE, high + AVG, relay_out)
         enter()
         pass_up().start()
+        answer()
         face_of(UP_FACE, high, up_out)
         up_face().start()
 
-    stage_moves(0)
+    @pl.when(member == 1)
+    def _():
+        stage_move(0, 1)
+        enter()
+        to_after(0).start()
+        stage_move(0, 0)
+        to_before(0).start()
+
+    @pl.when(member == 2)
+    def _():
+        stage_move(0, 0)
+        enter()
+        to_before(0).start()
+        stage_move(0, 1)
+        to_after(0).start()
+
+    @pl.when(jnp.logical_not(inner))
+    def _():
+        stage_moves(0)
+        move(0)
 
     @pl.when(inner)
     def _():
-        enter()
-
-    move(0)
-
-    @pl.when(inner)
-    def _():
+        answer()
         rest_loaded()
 
     @pl.when(member == 1)
@@ -562,7 +581,7 @@
                     done = 0
                     for half, x, size in runs:
                         if block < AVG or SPEEDS[d][2]:
-                            second[SLOT[d], block, half, pl.ds(x + 1, size), :] = post[d][done : done + size]
+                            second[SLOT[d], block, half, pl.ds(MAIN + x, size), :] = post[d][done : done + size]
                         done += size
 
     def finish(groups):
@@ -570,7 +589,7 @@
             known = {}
             for d in range(Q):
                 for runs in groups:
-                    value, done = streamed(second, d, block, runs, 1, known), 0
+                    value, done = streamed(second, d, block, runs, MAIN, known), 0
                     for half, x, size in runs:
                         at = (d * TILES + HALVES * x + half) * AVG + block
                         evolved[pl.ds(at, size, stride=AVG * HALVES), :] = value[done : done + size]
@@ -649,12 +668,12 @@
                 copy.wait_send()
 
         step([pairs(-1, 15, 2)])
-        finish(halves((0, 3), (13, 3)))
+        finish([pairs(0, 14, 2)])
 
     def core():
         settle(2)
         step([pairs(4, 10, 2)])
-        finish([pairs(3, 11, 2)])
+        finish(halves((2, 3), (11, 3)))
         settle(3)
         step([[(half, 6, 4) for half in range(HALVES)]])
         finish(halves((5, 6)))
@@ -721,7 +740,7 @@
             *boxes(2),
             *boxes(3),
             pltpu.VMEM((FIELDS, AVG + 1, HALVES, ROWS, LANES), f32),
-            pltpu.VMEM((FIELDS, AVG + 1, HALVES, NEXT_ROWS, LANES), f32),
+            pltpu.VMEM((FIELDS, AVG + 1, HALVES, ROWS, LANES), f32),
             *[faces() for _ in range(3)],
             *[faces(2) for _ in range(2)],
             *[faces() for _ in range(2)],

time: 14.7 us -> 14.7 us (level)
  no operation moved by 1% of the time
where the time goes in v7:
time: 14.7 us; the launch traced here: 14.6 us
  Pallas kernels  13.7 us (93%)
  local copies, waits for them, and re-layouts  0.83 us (6%)
    pallas_call x1, Pallas kernels, on_device(): pl.pallas_call(kernel, out_shape=jax.ShapeDtypeStruct((Q * TILES * AVG, L...  13.7 us
    unnamed x1, local copies, waits for them, and re-layouts  0.83 us

profile of v7, /device:TPU:1, one launch (start us, length us, event | category | flops | bytes accessed | tf_op | source)
XLA Modules:
  0.0 14.6 jit_solution(4316855166515012868)
XLA Ops:
  0.0 13.7 %shard_map.37 = f32[1216,128]{1,0:T(8,128)S(1)} custom-call(f32[19,128,128]{2,1,0:T(8,128)} %bitcast.19, f32[128,128]{1,0:T(8,128)} %bitcast.20, s32[1,4,8]{2,1,0:T(4,128)} %bitcast.21), custom_call_target="tpu_custom_call" | custom-call | flops 8000000 | bytes 3000000 | tf_op jit(solution)/shard_map/pallas_call | solution.py:731
  13.7 0.8 %copy.8 = f32[2,19,4096]{2,0,1:T(2,128)} copy(f32[2,19,4096]{2,0,1:T(2,128)S(1)} %bitcast.18) | data formatting | bytes 1245184
